TPU v7x, 256 devices: a whole 4x4x8 slice. The times are simulated.
256 devices in a mesh: prow: 8 (over x, core), pcol: 32 (over z, y).
Axes of the slice: x: 4, y: 4, z: 8, core: 2. Of those that a mesh axis runs over, the one named last changes fastest.
Arguments:
- kernel: float32 [8, 8, 256, 2, 32, 256], P(None, 'prow', None, None, 'pcol'), as said below
Outputs:
- factored: float32 [8, 8, 256, 2, 32, 256], P(None, 'prow', None, None, 'pcol')
Inputs may be any that keep to these rules, and one draw needn't show every extreme that they name: kernel read as a matrix is a symmetric positive definite covariance matrix.
All inputs are finite; a program needn't handle non-finite values.
Results may differ from a plain program's by a relative error of at most 0.0003.
Values sent between devices are 32-bit elements; how exact they have to be, the bound alone decides.
No kernel may reach another device: no remote copies, remote signals or barrier semaphores. Data moves between devices by JAX's collectives and lax.ppermute only.
A program may use at most 64 MiB of HBM per device.

v0:
```python
import jax
import jax.numpy as jnp
from jax import lax
from jax.sharding import PartitionSpec as P

STEPS = 2


def from_root(value, axis, source):
    kept = jnp.where(lax.axis_index(axis) == source, value, 0).astype(value.dtype)
    return lax.psum(kept, axis)


def per_device(kernel):
    shape = kernel.shape
    loc_rows, tile, loc_cols = (shape[0], shape[2], shape[3])
    row_count = lax.axis_size("prow")
    col_count = lax.axis_size("pcol")
    row_index = lax.axis_index("prow")
    col_index = lax.axis_index("pcol")
    ratio = col_count // row_count
    grow = jnp.arange(loc_rows * tile) // tile * row_count + row_index
    gcol = jnp.arange(loc_cols) * col_count + col_index
    identity = jnp.eye(tile, dtype=jnp.float32)
    blocks = kernel.reshape(loc_rows * tile, loc_cols, tile)

    def make_panel(column, section):
        block_row = section // row_count
        candidate = column[block_row * tile : (block_row + 1) * tile]
        diag_block = from_root(candidate, "prow", section % row_count)
        factor = jnp.linalg.cholesky(diag_block)
        inverse = jax.scipy.linalg.solve_triangular(factor, identity, lower=True)
        solved = jnp.dot(column, inverse.T, precision=lax.Precision.HIGHEST)
        stacked = jnp.tile(factor, (loc_rows, 1))
        piece = jnp.where(
            (grow > section)[:, None], solved, jnp.where((grow == section)[:, None], stacked, 0.0)
        )
        left_rows = from_root(piece, "pcol", section % col_count)
        grouped = left_rows.reshape(loc_cols, ratio, tile, tile)
        mine = lax.dynamic_index_in_dim(grouped, col_index // row_count, 1, keepdims=False)
        left_cols = from_root(mine, "prow", col_index % row_count)
        return (left_rows, left_cols)

    panels = make_panel(blocks[:, 0, :], 0)
    for section in range(STEPS):
        left_rows, left_cols = panels
        product = jnp.einsum("rk,mbk->rmb", left_rows, left_cols, precision=lax.Precision.HIGHEST)
        updated = blocks - product
        upper = (gcol > section)[None, :, None] & (grow <= section)[:, None, None]
        updated = jnp.where(upper, 0.0, updated)
        blocks = jnp.where((gcol == section)[None, :, None], left_rows[:, None, :], updated)
        if section + 1 < STEPS:
            panels = make_panel(blocks[:, (section + 1) // col_count, :], section + 1)
    return blocks.reshape(shape)


def solution(mesh):
    placed = (P(None, "prow", None, None, "pcol", None),)
    return jax.shard_map(
        per_device,
        mesh=mesh,
        in_specs=placed,
        out_specs=P(None, "prow", None, None, "pcol", None),
        check_vma=False,
    )
```

profile of v0, /device:TPU:1, one launch (start us, length us, event | category | flops | bytes accessed | tf_op | source)
XLA Modules:
  0.0 771.1 jit_solution(12305812874255659519)
XLA Ops:
  6.5 6.4 copy.23
  12.9 7.2 copy.20
  20.1 1.7 fusion.6
  22.3 66.3 %all-reduce.8.cloned.1.call-done = f32[256,256]{0,1:T(8,128)} async-done(((f32[256,256]{0,1:T(8,128)}), f32[256,256]{0,1:T(8,128)}) %all-reduce.8.cloned.1.call-update) | async-done | bytes 262160 | tf_op jit(solution)/shard_map/psum | solution.py:11
  90.6 11.7 %cholesky.130 = f32[128,128]{1,0:T(8,128)S(1)} custom-call(f32[128,128]{1,0:T(8,128)S(1)} %cholesky.194), custom_call_target="Cholesky" | custom-call | tf_op jit(solution)/shard_map/jit(cholesky)/cholesky | solution.py:31
  102.4 9.8 %custom-call.13 = f32[1,128,128]{1,2,0:T(8,128)S(1)} custom-call(f32[1,128,128]{2,1,0:T(8,128)S(1)} %get-tuple-element.54), custom_call_target="InvertDiagBlocksLowerTriangular" | custom-call | tf_op jit(solution)/shard_map/jit(cholesky)/cholesky | solution.py:31
  112.7 11.7 %cholesky.147 = f32[128,128]{1,0:T(8,128)S(1)} custom-call(f32[128,128]{1,0:T(8,128)S(1)} %convolution_subtract_fusion.3), custom_call_target="Cholesky" | custom-call | tf_op jit(solution)/shard_map/jit(cholesky)/cholesky | solution.py:31
  126.5 4.5 while.4
  127.7 1.4 bitcast_dynamic-update-slice_fusion.4
  129.7 1.4 bitcast_dynamic-update-slice_fusion.4
  131.1 19.7 %custom-call.14 = f32[2,128,128]{1,2,0:T(8,128)S(1)} custom-call(f32[2,128,128]{2,1,0:T(8,128)S(1)} %get-tuple-element.21), custom_call_target="InvertDiagBlocksLowerTriangular" | custom-call | tf_op jit(solution)/shard_map/jit(_solve_triangular)/triangular_solve | solution.py:32
  154.1 3.5 fusion.2
  157.7 151.1 %all-reduce.10.cloned.1.call-done = f32[2048,256]{0,1:T(8,128)} async-done(((f32[2048,256]{0,1:T(8,128)}), f32[2048,256]{0,1:T(8,128)}) %all-reduce.10.cloned.1.call-update) | async-done | bytes 2097168 | tf_op jit(solution)/shard_map/psum | solution.py:11
  308.8 3.6 reshape.175
  312.4 2.2 constant_dynamic-slice_fusion.3
  316.1 65.0 %all-reduce.12.cloned.1.call-done = f32[2,256,256]{2,1,0:T(8,128)} async-done(((f32[2,256,256]{2,1,0:T(8,128)}), f32[2,256,256]{2,1,0:T(8,128)}) %all-reduce.12.cloned.1.call-update) | async-done | bytes 524304 | tf_op jit(solution)/shard_map/psum | solution.py:11
  381.1 5.7 select_select_fusion.1
  386.8 2.0 copy-done
  389.8 64.0 %all-reduce.14.cloned.1.call-done = f32[256,256]{0,1:T(8,128)} async-done(((f32[256,256]{0,1:T(8,128)}), f32[256,256]{0,1:T(8,128)}) %all-reduce.14.cloned.1.call-update) | async-done | bytes 262160 | tf_op jit(solution)/shard_map/psum | solution.py:11
  455.9 11.7 %cholesky.164 = f32[128,128]{1,0:T(8,128)S(1)} custom-call(f32[128,128]{1,0:T(8,128)S(1)} %cholesky.197), custom_call_target="Cholesky" | custom-call | tf_op jit(solution)/shard_map/jit(cholesky)/cholesky | solution.py:31
  467.7 9.8 %custom-call.15 = f32[1,128,128]{1,2,0:T(8,128)S(1)} custom-call(f32[1,128,128]{2,1,0:T(8,128)S(1)} %get-tuple-element.50), custom_call_target="InvertDiagBlocksLowerTriangular" | custom-call | tf_op jit(solution)/shard_map/jit(cholesky)/cholesky | solution.py:31
  478.0 11.7 %cholesky.181 = f32[128,128]{1,0:T(8,128)S(1)} custom-call(f32[128,128]{1,0:T(8,128)S(1)} %convolution_subtract_fusion.2), custom_call_target="Cholesky" | custom-call | tf_op jit(solution)/shard_map/jit(cholesky)/cholesky | solution.py:31
  492.4 4.3 while.5
  496.7 19.7 %custom-call.16 = f32[2,128,128]{1,2,0:T(8,128)S(1)} custom-call(f32[2,128,128]{2,1,0:T(8,128)S(1)} %get-tuple-element.22), custom_call_target="InvertDiagBlocksLowerTriangular" | custom-call | tf_op jit(solution)/shard_map/jit(_solve_triangular)/triangular_solve | solution.py:32
  519.7 3.5 fusion
  523.4 151.2 %all-reduce.16.cloned.1.call-done = f32[2048,256]{0,1:T(8,128)} async-done(((f32[2048,256]{0,1:T(8,128)}), f32[2048,256]{0,1:T(8,128)}) %all-reduce.16.cloned.1.call-update) | async-done | bytes 2097168 | tf_op jit(solution)/shard_map/psum | solution.py:11
  674.5 3.9 reshape.176
  678.4 2.2 constant_dynamic-slice_fusion.2
  682.1 65.1 %all-reduce.18.cloned.1.call-done = f32[2,256,256]{2,1,0:T(8,128)} async-done(((f32[2,256,256]{2,1,0:T(8,128)}), f32[2,256,256]{2,1,0:T(8,128)}) %all-reduce.18.cloned.1.call-update) | async-done | bytes 524304 | tf_op jit(solution)/shard_map/psum | solution.py:11
  747.1 5.7 select_select_fusion
  752.9 3.9 copy.28
  756.7 7.2 copy.14
  (82 shorter events, 23.7 us)
Async XLA Ops:
  6.5 82.0 %all-reduce.8.cloned.1.call-start = ((), (), s32[]{:S(2)}) async-start(), calls=%async_computation | async-start | bytes 524288 | tf_op jit(solution)/shard_map/psum | solution.py:11
  21.8 286.9 %all-reduce.10.cloned.1.call-start = ((), (), s32[]{:S(2)}) async-start(), calls=%async_computation.1 | async-start | bytes 4194304 | tf_op jit(solution)/shard_map/psum | solution.py:11
  151.9 2.2 copy-start.2
  157.6 223.5 %all-reduce.12.cloned.1.call-start = ((), (), s32[]{:S(2)}) async-start(), calls=%async_computation.2 | async-start | bytes 1048576 | tf_op jit(solution)/shard_map/psum | solution.py:11
  312.4 68.7 %copy-start.3 = (f32[2048,256]{0,1:T(8,128)S(1)}, f32[2048,256]{0,1:T(8,128)}, u32[]{:S(2)}) copy-start(f32[2048,256]{0,1:T(8,128)} %all-reduce.10.cloned.1.call-done) | copy-start | bytes 6291460
  316.0 137.9 %all-reduce.14.cloned.1.call-start = ((), (), s32[]{:S(2)}) async-start(), calls=%async_computation.3 | async-start | bytes 524288 | tf_op jit(solution)/shard_map/psum | solution.py:11
  386.8 2.0 copy-start
  389.6 285.0 %all-reduce.16.cloned.1.call-start = ((), (), s32[]{:S(2)}) async-start(), calls=%async_computation.4 | async-start | bytes 4194304 | tf_op jit(solution)/shard_map/psum | solution.py:11
  517.6 2.2 copy-start.1
  523.3 223.8 %all-reduce.18.cloned.1.call-start = ((), (), s32[]{:S(2)}) async-start(), calls=%async_computation.5 | async-start | bytes 1048576 | tf_op jit(solution)/shard_map/psum | solution.py:11
  678.4 68.7 %copy-start.4 = (f32[2048,256]{0,1:T(8,128)S(1)}, f32[2048,256]{0,1:T(8,128)}, u32[]{:S(2)}) copy-start(f32[2048,256]{0,1:T(8,128)} %all-reduce.16.cloned.1.call-done) | copy-start | bytes 6291460
Sparse Core Ops, SparseCore 0:
  22.0 66.5 all-reduce.7
  157.7 151.0 all-reduce.9
  316.1 64.9 all-reduce.11
  389.7 64.0 all-reduce.13
  523.4 151.0 all-reduce.15
  682.1 65.0 all-reduce.17
where the time goes:
time: 776 us; the launch traced here: 771 us
  waiting for transfers between devices  563 us (73%)
  other arithmetic  114 us (15%)
  local copies, waits for them, and re-layouts  54.7 us (7%)
  matrix products  21.1 us (3%)
  between operations  16.7 us (2%)
    psum x6, waiting for transfers between devices, from_root(): return lax.psum(kept, axis)  563 us
    another operation x13, other arithmetic, make_panel(): factor = jnp.linalg.cholesky(diag_block)  68.6 us
    another operation x5, other arithmetic, make_panel(): inverse = jax.scipy.linalg.solve_triangular(factor, identity, lower=True)  39.4 us
    unnamed x16, local copies, waits for them, and re-layouts  17.6 us
  transfers between devices with their start and end apart: 6, of which 6 were waited for; matrix products, arithmetic and copies ran while one was open for 0% of the time, Pallas kernels for 0%

commit v1 on v0

v1 whole, which is shorter than its diff:
```python
import jax
import jax.numpy as jnp
from jax import lax
from jax.experimental import pallas as pl
from jax.experimental.pallas import tpu as pltpu
from jax.sharding import PartitionSpec as P

AXES = ("prow", "pcol")
ROWS, COLS = 8, 32
HIGHEST = lax.Precision.HIGHEST


def dot(a, b, dims=((1,), (0,))):
    return lax.dot_general(
        a, b, (dims, ((), ())), precision=HIGHEST, preferred_element_type=jnp.float32
    )


def send(value, pairs):
    flat = [(p * COLS + s, u * COLS + v) for (p, s), (u, v) in pairs]
    return lax.ppermute(value, AXES, flat)


def swap_cores(value):
    return send(value, [((p, s), (p ^ 1, s)) for p in range(ROWS) for s in range(COLS)])


def along_x(value, cols):
    parts = [
        send(value, [((p, s), (2 * k + p, s)) for p in range(2) for s in cols]) for k in (1, 2, 3)
    ]
    return value + (parts[0] + parts[1] + parts[2])


def along_y(value):
    parts = [send(value, [((p, 0), (p, k)) for p in range(ROWS)]) for k in (1, 2, 3)]
    return value + (parts[0] + parts[1] + parts[2])


def along_z(value):
    parts = [
        send(value, [((p, y), (p, 4 * k + y)) for p in range(ROWS) for y in range(4)])
        for k in range(1, 8)
    ]
    total = value
    for part in parts:
        total = total + part
    return total


def scatter_rows(own):
    parts = []
    for i in range(8):
        pairs = []
        for q in range(4):
            for t in range(8):
                s = 8 * q + t
                pairs.append(((0, s), (t, 8 * q + i)))
                pairs.append(((1, s), (t, 8 * q + (i + 4) % 8)))
        parts.append(send(own[128 * i : 128 * (i + 1)], pairs))
    low = (parts[0] + parts[1]) + (parts[2] + parts[3])
    high = (parts[4] + parts[5]) + (parts[6] + parts[7])
    return jnp.concatenate([low, high], axis=0)


def eliminate(block):
    sub = lax.broadcasted_iota(jnp.int32, (8, 128), 0)
    lane = lax.broadcasted_iota(jnp.int32, (8, 128), 1)
    left, right = [], []
    for i in range(16):
        left.append(block[8 * i : 8 * i + 8, :])
        right.append(jnp.where(lane == sub + 8 * i, 1.0, 0.0))
    for b in range(16):
        for j in range(8):
            c = 8 * b + j
            row_left, row_right = left[b][j : j + 1, :], right[b][j : j + 1, :]
            scale = 1.0 / row_left[:, c : c + 1]
            row_left, row_right = row_left * scale, row_right * scale
            for i in range(b, 16):
                if i == b and j == 7:
                    continue
                column = left[i][:, c : c + 1]
                if i == b:
                    column = jnp.where(sub[:, :1] > j, column, 0.0)
                left[i] = left[i] - column * row_left
                right[i] = right[i] - column * row_right
    upper, inverse = [], []
    for i in range(16):
        pivot = jnp.sum(jnp.where(lane == sub + 8 * i, left[i], 0.0), axis=1, keepdims=True)
        scale = lax.rsqrt(pivot)
        upper.append(jnp.where(lane >= sub + 8 * i, left[i] * scale, 0.0))
        inverse.append(right[i] * scale)
    return jnp.concatenate(upper, 0), jnp.concatenate(inverse, 0)


def factor_kernel(place, first, first_other, second, second_other, upper, inverse, work):
    odd = place[0] % 2 == 1
    for h in range(2):
        lanes = slice(128 * h, 128 * h + 128)
        far = slice(256 + 128 * h, 384 + 128 * h)
        mine = first[pl.ds(h, 128, stride=2), :]
        other = first_other[pl.ds(h, 128, stride=2), :]
        work[0:128, lanes] = jnp.where(odd, other, mine)
        work[128:256, lanes] = jnp.where(odd, mine, other)
        mine = second[pl.ds(h, 256, stride=2), :]
        other = second_other[pl.ds(h, 256, stride=2), :]
        work[0:256, far] = jnp.where(odd, other, mine)
        work[256:512, far] = jnp.where(odd, mine, other)
    work[256:512, 0:256] = jnp.zeros((256, 256), jnp.float32)
    row = lax.broadcasted_iota(jnp.int32, (512, 512), 0)
    col = lax.broadcasted_iota(jnp.int32, (512, 512), 1)
    work[:, 512:] = jnp.where(row == col, 1.0, 0.0)
    upper[...] = jnp.zeros((512, 512), jnp.float32)
    inverse[...] = jnp.zeros((512, 512), jnp.float32)
    for k in range(4):
        lo, hi = 128 * k, 128 * k + 128
        up, inv = eliminate(work[lo:hi, lo:hi])
        upper[lo:hi, lo:hi] = up
        inverse[lo:hi, lo:hi] = inv
        if k:
            inverse[lo:hi, :lo] = dot(inv, work[lo:hi, 512 : 512 + lo])
        if k < 3:
            right = dot(inv, work[lo:hi, hi:512])
            upper[lo:hi, hi:] = right
            work[hi:512, hi:512] -= dot(right, right, ((0,), (0,)))
            work[hi:512, 512 : 512 + hi] -= dot(right, inverse[lo:hi, :hi], ((0,), (0,)))


def factor(place, first, first_other, second, second_other):
    square = jax.ShapeDtypeStruct((512, 512), jnp.float32)
    vmem = pl.BlockSpec(memory_space=pltpu.VMEM)
    return pl.pallas_call(
        factor_kernel,
        out_shape=(square, square),
        in_specs=[pl.BlockSpec(memory_space=pltpu.SMEM)] + [vmem] * 4,
        out_specs=(vmem, vmem),
        scratch_shapes=[pltpu.VMEM((512, 1024), jnp.float32)],
        compiler_params=pltpu.CompilerParams(vmem_limit_bytes=32 << 20),
        cost_estimate=pl.CostEstimate(flops=40_000_000_000, bytes_accessed=4 << 20, transcendentals=0),
        name="factor",
    )(place, first, first_other, second, second_other)


def update_kernel(place, a, gathered, mine, other, upper, inverse, out, weight, lhs):
    r = pl.program_id(0)
    p, s = place[0], place[1]

    @pl.when(r == 0)
    def _():
        odd = p % 2 == 1
        for ch in range(4):
            lanes = slice(128 * ch, 128 * ch + 128)
            here, there = mine[pl.ds(ch, 256, stride=4), :], other[pl.ds(ch, 256, stride=4), :]
            weight[0:256, lanes] = jnp.where(odd, there, here)
            weight[256:512, lanes] = jnp.where(odd, here, there)
        half = dot(inverse[...], weight[...])
        row = lax.broadcasted_iota(jnp.int32, (512, 512), 0)
        col = lax.broadcasted_iota(jnp.int32, (512, 512), 1)
        pick = jnp.where(row == col + 256 * s, -1.0, 0.0)
        half = jnp.where((col < 256) & (s < 2), pick, half)
        weight[...] = dot(inverse[...], half, ((0,), (0,)))

    c, q = r // 4, r % 4
    for t in range(8):
        for slot in range(2):
            if t < 4:
                k = 32 * t if slot == 0 else 256 + 32 * (t + 4)
            else:
                k = 256 + 32 * (t - 4) if slot == 0 else 32 * t
            for h in range(2):
                start = q * 2048 + (t * 256 + slot * 128 + h) + 2 * c
                lhs[k : k + 32, 128 * h : 128 * h + 128] = gathered[pl.ds(start, 32, stride=4), :]
    product = dot(lhs[...], weight[...], ((0,), (0,)))
    for ch in range(4):
        kept = a[pl.ds(ch, 256, stride=4), :]
        if ch < 2:
            kept = jnp.where(s < 2, 0.0, kept)
        out[pl.ds(ch, 256, stride=4), :] = kept - product[:, 128 * ch : 128 * ch + 128]

    @pl.when((r == 0) & (p < 2))
    def _():
        for ch in range(4):
            where = pl.ds(ch, 256, stride=4)
            if ch >= 2:
                out[where, :] = jnp.zeros((256, 128), jnp.float32)
            else:
                lanes = slice(128 * ch, 128 * ch + 128)
                near = jnp.where(p == 0, upper[lanes, 0:256], upper[256 + 128 * ch : 384 + 128 * ch, 256:512])
                diagonal = near.T
                natural = out[where, :]
                out[where, :] = jnp.where(s == p, diagonal, jnp.where(s > p, 0.0, natural))


def update(place, a, gathered, mine, other, upper, inverse):
    vmem = pl.BlockSpec(memory_space=pltpu.VMEM)
    return pl.pallas_call(
        update_kernel,
        out_shape=jax.ShapeDtypeStruct(a.shape, jnp.float32),
        grid=(8,),
        in_specs=[
            pl.BlockSpec(memory_space=pltpu.SMEM),
            pl.BlockSpec((1024, 128), lambda r: (r, 0)),
            vmem,
            vmem,
            vmem,
            vmem,
            vmem,
        ],
        out_specs=pl.BlockSpec((1024, 128), lambda r: (r, 0)),
        scratch_shapes=[
            pltpu.VMEM((512, 512), jnp.float32),
            pltpu.VMEM((512, 256), jnp.float32),
        ],
        compiler_params=pltpu.CompilerParams(vmem_limit_bytes=40 << 20),
        cost_estimate=pl.CostEstimate(flops=8_000_000_000, bytes_accessed=16 << 20, transcendentals=0),
        name="update",
    )(place, a, gathered, mine, other, upper, inverse)


def per_device(kernel):
    p, s = lax.axis_index("prow"), lax.axis_index("pcol")
    place = jnp.stack([p, s]).astype(jnp.int32)
    a = kernel.reshape(8192, 128)
    own = a[:1024]

    gathered = lax.all_gather(scatter_rows(own), "pcol", tiled=True)

    block = own.reshape(256, 4, 128)[:, :2].reshape(512, 128)
    root = (p == 0) & (s == 0)
    first = send(block[256:], [((0, 0), (1, 0))])
    first = jnp.where(root, block[:256], first)
    first = along_z(along_y(along_x(first, (0,))))
    second = send(block, [((0, 1), (0, 0)), ((1, 1), (1, 0))])
    second = along_z(along_y(along_x(second, (0,))))
    upper, inverse = factor(place, first, swap_cores(first), second, swap_cores(second))

    mine = along_x(jnp.where(p < 2, own, 0.0), range(COLS))
    other = swap_cores(mine)
    out = update(place, a, gathered, mine, other, upper, inverse)
    return out.reshape(kernel.shape)


def solution(mesh):
    spec = P(None, "prow", None, None, "pcol", None)
    return jax.shard_map(per_device, mesh=mesh, in_specs=(spec,), out_specs=spec, check_vma=False)
```

time: 776 us -> 198 us (0.26)
  waiting for transfers between devices: 563 us -> 19.2 us
  other arithmetic: 114 us -> 2.92 us
  starting transfers between devices: 0.71 us -> 94.2 us
  Pallas kernels: 0 us -> 60.2 us
  local copies, waits for them, and re-layouts: 54.7 us -> 5.98 us
  matrix products: 21.1 us -> 0 us
    psum x6 -> x0, waiting for transfers between devices: 563 us -> none  [from_root(): return lax.psum(kept, axis)]
    another operation x18 -> x1, other arithmetic: 108 us -> 0.08 us  [per_device(): place = jnp.stack([p, s]).astype(jnp.int32)]
    ppermute x0 -> x42, starting transfers between devices: none -> 94.2 us  [send(): return lax.ppermute(value, AXES, flat)]
    pallas_call x0 -> x2, Pallas kernels: none -> 60.2 us  [the longest x1 46.3 us: factor(): pl.pallas_call(factor_kernel, out_shape=(square, square), in_specs=[pl.Bl...]
    reshape x4 -> x0, local copies, waits for them, and re-layouts: 22 us -> none  [the longest x2 7.49 us: make_panel(): grouped = left_rows.reshape(loc_cols, ratio, tile, tile)]
    ppermute x0 -> x42, waiting for transfers between devices: none -> 19.1 us  [send(): return lax.ppermute(value, AXES, flat)]
    dot_general x4 -> x0, matrix products: 18.4 us -> none  [the longest x2 11.4 us: per_device(): jnp.einsum('rk,mbk->rmb', left_rows, left_cols, precision=lax.Precision.H...]
    unnamed x16 -> x4, local copies, waits for them, and re-layouts: 17.6 us -> 4.37 us
  transfers between devices with their start and end apart: 6 -> 43, of which waited for: 6 -> 10; matrix products, arithmetic and copies ran while one was open for 0% -> 1% of each run, Pallas kernels for 0% -> 24%
where the time goes in v1:
time: 198 us; the launch traced here: 197 us
  starting transfers between devices  94.2 us (48%)
  Pallas kernels  60.2 us (30%)
  waiting for transfers between devices  19.2 us (10%)
  between operations  14 us (7%)
  local copies, waits for them, and re-layouts  5.98 us (3%)
  other arithmetic  2.92 us (1%)
    ppermute x42, starting transfers between devices, send(): return lax.ppermute(value, AXES, flat)  94.2 us
    pallas_call x1, Pallas kernels, factor(): pl.pallas_call(factor_kernel, out_shape=(square, square), in_specs=[pl.Bl...  46.3 us
    ppermute x42, waiting for transfers between devices, send(): return lax.ppermute(value, AXES, flat)  19.1 us
    pallas_call x1, Pallas kernels, update(): pl.pallas_call(update_kernel, out_shape=jax.ShapeDtypeStruct(a.shape, jnp...  13.9 us
    unnamed x4, local copies, waits for them, and re-layouts  4.37 us
  transfers between devices with their start and end apart: 43, of which 10 were waited for; matrix products, arithmetic and copies ran while one was open for 1% of the time, Pallas kernels for 24%

profile of v1, /device:TPU:1, one launch (start us, length us, event | category | flops | bytes accessed | tf_op | source)
XLA Modules:
  0.0 196.5 jit_solution(16438458723708349629)
XLA Ops:
  6.5 1.4 fusion.1
  8.0 5.9 %collective-permute-start.1 = (f32[128,128]{1,0:T(8,128)S(1)}, f32[128,128]{1,0:T(8,128)S(1)}, u32[]{:S(2)}, u32[]{:S(2)}) collective-permute-start(f32[128,128]{1,0:T(8,128)S(1)} %bitcast.34), channel_id=1, source_target_pairs={{0,1},{32,5},{1,33},{33,37},{2,65},{34,69},{3,97},{35,101},{4,129}... | collective-permute-start | bytes 196616 | tf_op jit(solution)/shard_map/ppermute | solution.py:21
  13.9 5.8 %collective-permute-start.3 = (f32[128,128]{1,0:T(8,128)S(1)}, f32[128,128]{1,0:T(8,128)S(1)}, u32[]{:S(2)}, u32[]{:S(2)}) collective-permute-start(f32[128,128]{1,0:T(8,128)S(1)} %bitcast.33), channel_id=1, source_target_pairs={{0,3},{32,7},{1,35},{33,39},{2,67},{34,71},{3,99},{35,103},{4,131}... | collective-permute-start | bytes 196616 | tf_op jit(solution)/shard_map/ppermute | solution.py:21
  19.7 1.5 collective-permute-start.2
  21.2 1.9 collective-permute-start
  24.4 3.6 %collective-permute-start.5 = (f32[128,128]{1,0:T(8,128)S(1)}, f32[128,128]{1,0:T(8,128)S(1)}, u32[]{:S(2)}, u32[]{:S(2)}) collective-permute-start(f32[128,128]{1,0:T(8,128)S(1)} %bitcast.29), channel_id=1, source_target_pairs={{0,5},{32,1},{1,37},{33,33},{2,69},{34,65},{3,101},{35,97},{4,133}... | collective-permute-start | bytes 196616 | tf_op jit(solution)/shard_map/ppermute | solution.py:21
  28.1 1.9 collective-permute-start.4
  31.4 1.7 collective-permute-done.4
  33.8 1.7 fusion
  42.7 2.8 %collective-permute-done.27 = f32[512,128]{1,0:T(8,128)S(1)} collective-permute-done((f32[512,128]{1,0:T(8,128)S(1)}, f32[512,128]{1,0:T(8,128)S(1)}, u32[]{:S(2)}, u32[]{:S(2)}) %collective-permute-start.27) | collective-permute-done | bytes 262176 | tf_op jit(solution)/shard_map/ppermute | solution.py:21
  46.8 1.3 collective-permute-start.29
  48.2 1.3 collective-permute-start.28
  53.5 4.1 %collective-permute-done.28 = f32[512,128]{1,0:T(8,128)S(1)} collective-permute-done((f32[512,128]{1,0:T(8,128)S(1)}, f32[512,128]{1,0:T(8,128)S(1)}, u32[]{:S(2)}, u32[]{:S(2)}) %collective-permute-start.28) | collective-permute-done | bytes 262176 | tf_op jit(solution)/shard_map/ppermute | solution.py:21
  57.6 1.3 collective-permute-start.33
  58.9 1.3 collective-permute-start.32
  60.2 1.3 collective-permute-start.31
  66.1 1.4 collective-permute-done.24
  72.9 1.3 collective-permute-start.40
  74.2 2.8 %collective-permute-start.39 = (f32[512,128]{1,0:T(8,128)S(1)}, f32[512,128]{1,0:T(8,128)S(1)}, u32[]{:S(2)}, u32[]{:S(2)}) collective-permute-start(f32[512,128]{1,0:T(8,128)S(1)} %add_add_fusion.2), channel_id=1, source_target_pairs={{0,24},{1,25},{2,26},{3,27},{32,56},{33,57},{34,58},{35,59},{64,88... | collective-permute-start | bytes 786440 | tf_op jit(solution)/shard_map/ppermute | solution.py:21
  77.0 2.2 %collective-permute-start.38 = (f32[512,128]{1,0:T(8,128)S(1)}, f32[512,128]{1,0:T(8,128)S(1)}, u32[]{:S(2)}, u32[]{:S(2)}) collective-permute-start(f32[512,128]{1,0:T(8,128)S(1)} %add_add_fusion.2), channel_id=1, source_target_pairs={{0,20},{1,21},{2,22},{3,23},{32,52},{33,53},{34,54},{35,55},{64,84... | collective-permute-start | bytes 786440 | tf_op jit(solution)/shard_map/ppermute | solution.py:21
  80.5 1.3 collective-permute-start.36
  84.6 2.5 %collective-permute-done.38 = f32[512,128]{1,0:T(8,128)S(1)} collective-permute-done((f32[512,128]{1,0:T(8,128)S(1)}, f32[512,128]{1,0:T(8,128)S(1)}, u32[]{:S(2)}, u32[]{:S(2)}) %collective-permute-start.38) | collective-permute-done | bytes 262176 | tf_op jit(solution)/shard_map/ppermute | solution.py:21
  87.1 1.3 collective-permute-start.10
  88.5 1.3 collective-permute-start.9
  90.0 6.5 %collective-permute-start.8 = (f32[1024,128]{1,0:T(8,128)S(1)}, f32[1024,128]{1,0:T(8,128)S(1)}, u32[]{:S(2)}, u32[]{:S(2)}) collective-permute-start(f32[1024,128]{1,0:T(8,128)S(1)} %bitcast.20), channel_id=1, source_target_pairs={{0,64},{1,65},{2,66},{3,67},{4,68},{5,69},{6,70},{7,71},{8,72},{9,... | collective-permute-start | bytes 1572872 | tf_op jit(solution)/shard_map/ppermute | solution.py:21
  96.6 4.4 %collective-permute-done.35 = f32[512,128]{1,0:T(8,128)S(1)} collective-permute-done((f32[512,128]{1,0:T(8,128)S(1)}, f32[512,128]{1,0:T(8,128)S(1)}, u32[]{:S(2)}, u32[]{:S(2)}) %collective-permute-start.35) | collective-permute-done | bytes 262176 | tf_op jit(solution)/shard_map/ppermute | solution.py:21
  101.0 18.2 %collective-permute-start.26 = (f32[256,128]{1,0:T(8,128)S(1)}, f32[256,128]{1,0:T(8,128)S(1)}, u32[]{:S(2)}, u32[]{:S(2)}) collective-permute-start(f32[256,128]{1,0:T(8,128)S(1)} %add_add_fusion.4.first), channel_id=1, source_target_pairs={{0,32},{1,33},{2,34},{3,35},{4,36},{5,37},{6,38},{7,39},{8,40},{9,... | collective-permute-start | bytes 393224 | tf_op jit(solution)/shard_map/ppermute | solution.py:21
  119.3 4.6 %collective-permute-start.41 = (f32[512,128]{1,0:T(8,128)S(1)}, f32[512,128]{1,0:T(8,128)S(1)}, u32[]{:S(2)}, u32[]{:S(2)}) collective-permute-start(f32[512,128]{1,0:T(8,128)S(1)} %add_add_fusion.1.second), channel_id=1, source_target_pairs={{0,32},{1,33},{2,34},{3,35},{4,36},{5,37},{6,38},{7,39},{8,40},{9,... | collective-permute-start | bytes 786440 | tf_op jit(solution)/shard_map/ppermute | solution.py:21
  125.1 46.3 %factor.1 = (f32[512,512]{1,0:T(8,128)S(1)}, f32[512,512]{1,0:T(8,128)S(1)}) custom-call(s32[2]{0:T(128)S(1)} %pad_add_fusion.place, f32[256,128]{1,0:T(8,128)S(1)} %add_add_fusion.4.first, f32[256,128]{1,0:T(8,128)S(1)} %collective-permute-done.26.first_other, f32[512,128]{1,0:T(8,128)S(1)} %add_add_fusion.1.second, ...), custom_call_target="tpu_custom_call" | custom-call | flops 40000000000 | bytes 4194304 | tf_op jit(solution)/shard_map/factor/pallas_call | solution.py:132
  171.5 2.2 %copy-done = f32[8,1,256,2,1,256]{5,4,3,2,1,0:T(1,128)S(1)} copy-done((f32[8,1,256,2,1,256]{5,4,3,2,1,0:T(1,128)S(1)}, f32[8,1,256,2,1,256]{5,4,3,2,1,0:T(1,128)}, u32[]{:S(2)}) %copy-start) | copy-done | bytes 4194328
  173.6 2.2 %copy-done.1 = f32[8192,128]{1,0:T(8,128)S(1)} copy-done((f32[8192,128]{1,0:T(8,128)S(1)}, f32[8192,128]{1,0:T(8,128)}, u32[]{:S(2)}) %copy-start.1) | copy-done | bytes 4194328
  175.8 13.9 %update.1 = f32[8192,128]{1,0:T(8,128)} custom-call(s32[2]{0:T(128)S(1)} %pad_add_fusion.place, f32[8192,128]{1,0:T(8,128)S(1)} %bitcast.17, f32[8192,128]{1,0:T(8,128)S(1)} %copy-done.1, f32[1024,128]{1,0:T(8,128)S(1)} %add_add_fusion.mine, f32[1024,128]{1,0:T(8,128)S(1)} %collective-permute-done.11.other, f32[512,512]{1,0:T(8,128)S(1)} %get-tuple-element.7.upper, ...), custom_call_target="tpu_custom_call" | custom-call | flops 8000000000 | bytes 16777216 | tf_op jit(solution)/shard_map/update/pallas_call | solution.py:196
  (77 shorter events, 31.2 us)
Async XLA Ops:
  6.5 164.9 %all-gather.2.cloned.1.call-start = ((), (), s32[]{:S(2)}) async-start(), calls=%async_computation | async-start | bytes 4325376 | tf_op jit(solution)/shard_map/all_gather | solution.py:226
  8.0 16.4 %collective-permute-start.1 = (f32[128,128]{1,0:T(8,128)S(1)}, f32[128,128]{1,0:T(8,128)S(1)}, u32[]{:S(2)}, u32[]{:S(2)}) collective-permute-start(f32[128,128]{1,0:T(8,128)S(1)} %bitcast.34), channel_id=1, source_target_pairs={{0,1},{32,5},{1,33},{33,37},{2,65},{34,69},{3,97},{35,101},{4,129}... | collective-permute-start | bytes 196616 | tf_op jit(solution)/shard_map/ppermute | solution.py:21
  13.9 14.1 %collective-permute-start.3 = (f32[128,128]{1,0:T(8,128)S(1)}, f32[128,128]{1,0:T(8,128)S(1)}, u32[]{:S(2)}, u32[]{:S(2)}) collective-permute-start(f32[128,128]{1,0:T(8,128)S(1)} %bitcast.33), channel_id=1, source_target_pairs={{0,3},{32,7},{1,35},{33,39},{2,67},{34,71},{3,99},{35,103},{4,131}... | collective-permute-start | bytes 196616 | tf_op jit(solution)/shard_map/ppermute | solution.py:21
  19.7 10.3 %collective-permute-start.2 = (f32[128,128]{1,0:T(8,128)S(1)}, f32[128,128]{1,0:T(8,128)S(1)}, u32[]{:S(2)}, u32[]{:S(2)}) collective-permute-start(f32[128,128]{1,0:T(8,128)S(1)} %bitcast.32), channel_id=1, source_target_pairs={{0,2},{32,6},{1,34},{33,38},{2,66},{34,70},{3,98},{35,102},{4,130}... | collective-permute-start | bytes 196616 | tf_op jit(solution)/shard_map/ppermute | solution.py:21
  21.2 10.1 %collective-permute-start = (f32[128,128]{1,0:T(8,128)S(1)}, f32[128,128]{1,0:T(8,128)S(1)}, u32[]{:S(2)}, u32[]{:S(2)}) collective-permute-start(f32[128,128]{1,0:T(8,128)S(1)} %bitcast.31), channel_id=1, source_target_pairs={{0,0},{32,4},{1,32},{33,36},{2,64},{34,68},{3,96},{35,100},{4,128}... | collective-permute-start | bytes 196616 | tf_op jit(solution)/shard_map/ppermute | solution.py:21
  23.1 8.2 %collective-permute-start.6 = (f32[128,128]{1,0:T(8,128)S(1)}, f32[128,128]{1,0:T(8,128)S(1)}, u32[]{:S(2)}, u32[]{:S(2)}) collective-permute-start(f32[128,128]{1,0:T(8,128)S(1)} %bitcast.30), channel_id=1, source_target_pairs={{0,6},{32,2},{1,38},{33,34},{2,70},{34,66},{3,102},{35,98},{4,134}... | collective-permute-start | bytes 196616 | tf_op jit(solution)/shard_map/ppermute | solution.py:21
  37.0 8.6 %collective-permute-start.27 = (f32[512,128]{1,0:T(8,128)S(1)}, f32[512,128]{1,0:T(8,128)S(1)}, u32[]{:S(2)}, u32[]{:S(2)}) collective-permute-start(f32[512,128]{1,0:T(8,128)S(1)} %bitcast.25), channel_id=1, source_target_pairs={{1,0},{33,32}} | collective-permute-start | bytes 786440 | tf_op jit(solution)/shard_map/ppermute | solution.py:21
  38.8 9.3 %collective-permute-start.15 = (f32[256,128]{1,0:T(8,128)S(1)}, f32[256,128]{1,0:T(8,128)S(1)}, u32[]{:S(2)}, u32[]{:S(2)}) collective-permute-start(f32[256,128]{1,0:T(8,128)S(1)} %broadcast_select_fusion.1), channel_id=1, source_target_pairs={{0,192},{32,224}} | collective-permute-start | bytes 393224 | tf_op jit(solution)/shard_map/ppermute | solution.py:21
  40.1 9.3 %collective-permute-start.14 = (f32[256,128]{1,0:T(8,128)S(1)}, f32[256,128]{1,0:T(8,128)S(1)}, u32[]{:S(2)}, u32[]{:S(2)}) collective-permute-start(f32[256,128]{1,0:T(8,128)S(1)} %broadcast_select_fusion.1), channel_id=1, source_target_pairs={{0,128},{32,160}} | collective-permute-start | bytes 393224 | tf_op jit(solution)/shard_map/ppermute | solution.py:21
  41.4 8.0 %collective-permute-start.13 = (f32[256,128]{1,0:T(8,128)S(1)}, f32[256,128]{1,0:T(8,128)S(1)}, u32[]{:S(2)}, u32[]{:S(2)}) collective-permute-start(f32[256,128]{1,0:T(8,128)S(1)} %broadcast_select_fusion.1), channel_id=1, source_target_pairs={{0,64},{32,96}} | collective-permute-start | bytes 393224 | tf_op jit(solution)/shard_map/ppermute | solution.py:21
  48.2 9.4 %collective-permute-start.28 = (f32[512,128]{1,0:T(8,128)S(1)}, f32[512,128]{1,0:T(8,128)S(1)}, u32[]{:S(2)}, u32[]{:S(2)}) collective-permute-start(f32[512,128]{1,0:T(8,128)S(1)} %collective-permute-done.27), channel_id=1, source_target_pairs={{0,64},{32,96}} | collective-permute-start | bytes 786440 | tf_op jit(solution)/shard_map/ppermute | solution.py:21
  49.5 10.7 %collective-permute-start.18 = (f32[256,128]{1,0:T(8,128)S(1)}, f32[256,128]{1,0:T(8,128)S(1)}, u32[]{:S(2)}, u32[]{:S(2)}) collective-permute-start(f32[256,128]{1,0:T(8,128)S(1)} %add_add_fusion.6), channel_id=1, source_target_pairs={{0,3},{32,35},{64,67},{96,99},{128,131},{160,163},{192,195},{224,2... | collective-permute-start | bytes 393224 | tf_op jit(solution)/shard_map/ppermute | solution.py:21
  50.8 10.7 %collective-permute-start.17 = (f32[256,128]{1,0:T(8,128)S(1)}, f32[256,128]{1,0:T(8,128)S(1)}, u32[]{:S(2)}, u32[]{:S(2)}) collective-permute-start(f32[256,128]{1,0:T(8,128)S(1)} %add_add_fusion.6), channel_id=1, source_target_pairs={{0,2},{32,34},{64,66},{96,98},{128,130},{160,162},{192,194},{224,2... | collective-permute-start | bytes 393224 | tf_op jit(solution)/shard_map/ppermute | solution.py:21
  52.1 9.4 %collective-permute-start.16 = (f32[256,128]{1,0:T(8,128)S(1)}, f32[256,128]{1,0:T(8,128)S(1)}, u32[]{:S(2)}, u32[]{:S(2)}) collective-permute-start(f32[256,128]{1,0:T(8,128)S(1)} %add_add_fusion.6), channel_id=1, source_target_pairs={{0,1},{32,33},{64,65},{96,97},{128,129},{160,161},{192,193},{224,2... | collective-permute-start | bytes 393224 | tf_op jit(solution)/shard_map/ppermute | solution.py:21
  57.6 11.2 %collective-permute-start.33 = (f32[512,128]{1,0:T(8,128)S(1)}, f32[512,128]{1,0:T(8,128)S(1)}, u32[]{:S(2)}, u32[]{:S(2)}) collective-permute-start(f32[512,128]{1,0:T(8,128)S(1)} %add_add_fusion.3), channel_id=1, source_target_pairs={{0,3},{32,35},{64,67},{96,99},{128,131},{160,163},{192,195},{224,2... | collective-permute-start | bytes 786440 | tf_op jit(solution)/shard_map/ppermute | solution.py:21
  58.9 11.2 %collective-permute-start.32 = (f32[512,128]{1,0:T(8,128)S(1)}, f32[512,128]{1,0:T(8,128)S(1)}, u32[]{:S(2)}, u32[]{:S(2)}) collective-permute-start(f32[512,128]{1,0:T(8,128)S(1)} %add_add_fusion.3), channel_id=1, source_target_pairs={{0,2},{32,34},{64,66},{96,98},{128,130},{160,162},{192,194},{224,2... | collective-permute-start | bytes 786440 | tf_op jit(solution)/shard_map/ppermute | solution.py:21
  60.2 11.2 %collective-permute-start.31 = (f32[512,128]{1,0:T(8,128)S(1)}, f32[512,128]{1,0:T(8,128)S(1)}, u32[]{:S(2)}, u32[]{:S(2)}) collective-permute-start(f32[512,128]{1,0:T(8,128)S(1)} %add_add_fusion.3), channel_id=1, source_target_pairs={{0,1},{32,33},{64,65},{96,97},{128,129},{160,161},{192,193},{224,2... | collective-permute-start | bytes 786440 | tf_op jit(solution)/shard_map/ppermute | solution.py:21
  68.9 8.1 %collective-permute-start.21 = (f32[256,128]{1,0:T(8,128)S(1)}, f32[256,128]{1,0:T(8,128)S(1)}, u32[]{:S(2)}, u32[]{:S(2)}) collective-permute-start(f32[256,128]{1,0:T(8,128)S(1)} %add_add_fusion.5), channel_id=1, source_target_pairs={{0,12},{1,13},{2,14},{3,15},{32,44},{33,45},{34,46},{35,47},{64,76... | collective-permute-start | bytes 393224 | tf_op jit(solution)/shard_map/ppermute | solution.py:21
  70.2 9.0 %collective-permute-start.20 = (f32[256,128]{1,0:T(8,128)S(1)}, f32[256,128]{1,0:T(8,128)S(1)}, u32[]{:S(2)}, u32[]{:S(2)}) collective-permute-start(f32[256,128]{1,0:T(8,128)S(1)} %add_add_fusion.5), channel_id=1, source_target_pairs={{0,8},{1,9},{2,10},{3,11},{32,40},{33,41},{34,42},{35,43},{64,72},... | collective-permute-start | bytes 393224 | tf_op jit(solution)/shard_map/ppermute | solution.py:21
  71.5 9.0 %collective-permute-start.19 = (f32[256,128]{1,0:T(8,128)S(1)}, f32[256,128]{1,0:T(8,128)S(1)}, u32[]{:S(2)}, u32[]{:S(2)}) collective-permute-start(f32[256,128]{1,0:T(8,128)S(1)} %add_add_fusion.5), channel_id=1, source_target_pairs={{0,4},{1,5},{2,6},{3,7},{32,36},{33,37},{34,38},{35,39},{64,68},{6... | collective-permute-start | bytes 393224 | tf_op jit(solution)/shard_map/ppermute | solution.py:21
  72.9 9.0 %collective-permute-start.40 = (f32[512,128]{1,0:T(8,128)S(1)}, f32[512,128]{1,0:T(8,128)S(1)}, u32[]{:S(2)}, u32[]{:S(2)}) collective-permute-start(f32[512,128]{1,0:T(8,128)S(1)} %add_add_fusion.2), channel_id=1, source_target_pairs={{0,28},{1,29},{2,30},{3,31},{32,60},{33,61},{34,62},{35,63},{64,92... | collective-permute-start | bytes 786440 | tf_op jit(solution)/shard_map/ppermute | solution.py:21
  74.2 9.0 %collective-permute-start.39 = (f32[512,128]{1,0:T(8,128)S(1)}, f32[512,128]{1,0:T(8,128)S(1)}, u32[]{:S(2)}, u32[]{:S(2)}) collective-permute-start(f32[512,128]{1,0:T(8,128)S(1)} %add_add_fusion.2), channel_id=1, source_target_pairs={{0,24},{1,25},{2,26},{3,27},{32,56},{33,57},{34,58},{35,59},{64,88... | collective-permute-start | bytes 786440 | tf_op jit(solution)/shard_map/ppermute | solution.py:21
  77.0 10.1 %collective-permute-start.38 = (f32[512,128]{1,0:T(8,128)S(1)}, f32[512,128]{1,0:T(8,128)S(1)}, u32[]{:S(2)}, u32[]{:S(2)}) collective-permute-start(f32[512,128]{1,0:T(8,128)S(1)} %add_add_fusion.2), channel_id=1, source_target_pairs={{0,20},{1,21},{2,22},{3,23},{32,52},{33,53},{34,54},{35,55},{64,84... | collective-permute-start | bytes 786440 | tf_op jit(solution)/shard_map/ppermute | solution.py:21
  79.2 9.2 %collective-permute-start.37 = (f32[512,128]{1,0:T(8,128)S(1)}, f32[512,128]{1,0:T(8,128)S(1)}, u32[]{:S(2)}, u32[]{:S(2)}) collective-permute-start(f32[512,128]{1,0:T(8,128)S(1)} %add_add_fusion.2), channel_id=1, source_target_pairs={{0,16},{1,17},{2,18},{3,19},{32,48},{33,49},{34,50},{35,51},{64,80... | collective-permute-start | bytes 786440 | tf_op jit(solution)/shard_map/ppermute | solution.py:21
  80.5 9.5 %collective-permute-start.36 = (f32[512,128]{1,0:T(8,128)S(1)}, f32[512,128]{1,0:T(8,128)S(1)}, u32[]{:S(2)}, u32[]{:S(2)}) collective-permute-start(f32[512,128]{1,0:T(8,128)S(1)} %add_add_fusion.2), channel_id=1, source_target_pairs={{0,12},{1,13},{2,14},{3,15},{32,44},{33,45},{34,46},{35,47},{64,76... | collective-permute-start | bytes 786440 | tf_op jit(solution)/shard_map/ppermute | solution.py:21
  81.9 19.1 %collective-permute-start.35 = (f32[512,128]{1,0:T(8,128)S(1)}, f32[512,128]{1,0:T(8,128)S(1)}, u32[]{:S(2)}, u32[]{:S(2)}) collective-permute-start(f32[512,128]{1,0:T(8,128)S(1)} %add_add_fusion.2), channel_id=1, source_target_pairs={{0,8},{1,9},{2,10},{3,11},{32,40},{33,41},{34,42},{35,43},{64,72},... | collective-permute-start | bytes 786440 | tf_op jit(solution)/shard_map/ppermute | solution.py:21
  83.2 36.0 %collective-permute-start.34 = (f32[512,128]{1,0:T(8,128)S(1)}, f32[512,128]{1,0:T(8,128)S(1)}, u32[]{:S(2)}, u32[]{:S(2)}) collective-permute-start(f32[512,128]{1,0:T(8,128)S(1)} %add_add_fusion.2), channel_id=1, source_target_pairs={{0,4},{1,5},{2,6},{3,7},{32,36},{33,37},{34,38},{35,39},{64,68},{6... | collective-permute-start | bytes 786440 | tf_op jit(solution)/shard_map/ppermute | solution.py:21
  87.1 36.8 %collective-permute-start.10 = (f32[1024,128]{1,0:T(8,128)S(1)}, f32[1024,128]{1,0:T(8,128)S(1)}, u32[]{:S(2)}, u32[]{:S(2)}) collective-permute-start(f32[1024,128]{1,0:T(8,128)S(1)} %bitcast.18), channel_id=1, source_target_pairs={{0,192},{1,193},{2,194},{3,195},{4,196},{5,197},{6,198},{7,199},{8... | collective-permute-start | bytes 1572872 | tf_op jit(solution)/shard_map/ppermute | solution.py:21
  88.5 35.5 %collective-permute-start.9 = (f32[1024,128]{1,0:T(8,128)S(1)}, f32[1024,128]{1,0:T(8,128)S(1)}, u32[]{:S(2)}, u32[]{:S(2)}) collective-permute-start(f32[1024,128]{1,0:T(8,128)S(1)} %bitcast.19), channel_id=1, source_target_pairs={{0,128},{1,129},{2,130},{3,131},{4,132},{5,133},{6,134},{7,135},{8... | collective-permute-start | bytes 1572872 | tf_op jit(solution)/shard_map/ppermute | solution.py:21
  90.0 33.9 %collective-permute-start.8 = (f32[1024,128]{1,0:T(8,128)S(1)}, f32[1024,128]{1,0:T(8,128)S(1)}, u32[]{:S(2)}, u32[]{:S(2)}) collective-permute-start(f32[1024,128]{1,0:T(8,128)S(1)} %bitcast.20), channel_id=1, source_target_pairs={{0,64},{1,65},{2,66},{3,67},{4,68},{5,69},{6,70},{7,71},{8,72},{9,... | collective-permute-start | bytes 1572872 | tf_op jit(solution)/shard_map/ppermute | solution.py:21
  101.0 23.3 %collective-permute-start.26 = (f32[256,128]{1,0:T(8,128)S(1)}, f32[256,128]{1,0:T(8,128)S(1)}, u32[]{:S(2)}, u32[]{:S(2)}) collective-permute-start(f32[256,128]{1,0:T(8,128)S(1)} %add_add_fusion.4.first), channel_id=1, source_target_pairs={{0,32},{1,33},{2,34},{3,35},{4,36},{5,37},{6,38},{7,39},{8,40},{9,... | collective-permute-start | bytes 393224 | tf_op jit(solution)/shard_map/ppermute | solution.py:21
  124.0 47.4 %collective-permute-start.11 = (f32[1024,128]{1,0:T(8,128)S(1)}, f32[1024,128]{1,0:T(8,128)S(1)}, u32[]{:S(2)}, u32[]{:S(2)}) collective-permute-start(f32[1024,128]{1,0:T(8,128)S(1)} %add_add_fusion.mine), channel_id=1, source_target_pairs={{0,32},{1,33},{2,34},{3,35},{4,36},{5,37},{6,38},{7,39},{8,40},{9,... | collective-permute-start | bytes 1572872 | tf_op jit(solution)/shard_map/ppermute | solution.py:21
  (13 other events, 64.2 us)
Sparse Core Ops, SparseCore 0:
  33.9 87.9 all-gather.1

commit v2 on v1

v2 whole, which is shorter than its diff:
```python
import jax
import jax.numpy as jnp
from jax import lax
from jax.experimental import pallas as pl
from jax.experimental.pallas import tpu as pltpu
from jax.sharding import PartitionSpec as P

AXES = ("prow", "pcol")
ROWS, COLS = 8, 32
HIGHEST = lax.Precision.HIGHEST


def dot(a, b, dims=((1,), (0,))):
    return lax.dot_general(
        a, b, (dims, ((), ())), precision=HIGHEST, preferred_element_type=jnp.float32
    )


def send(value, pairs):
    flat = [(p * COLS + s, u * COLS + v) for (p, s), (u, v) in pairs]
    return lax.ppermute(value, AXES, flat)


def swap_cores(value):
    return send(value, [((p, s), (p ^ 1, s)) for p in range(ROWS) for s in range(COLS)])


def shifted(value, dx=0, dy=0, dz=0, keep=lambda p, s: True):
    pairs = []
    for p in range(ROWS):
        for s in range(COLS):
            if keep(p, s):
                z, y = divmod(s, 4)
                pairs.append(
                    ((p, s), ((p + 2 * dx) % ROWS, (z + dz) % 8 * 4 + (y + dy) % 4))
                )
    return send(value, pairs)


def after(value, *others):
    return lax.optimization_barrier((value, *others))[0]


def together(*values):
    return lax.optimization_barrier(values)


def stage(value, index, cores=(0, 1), root_y=0):
    moves, at_x, at_y, at_z = (
        ([{"dy": 1}, {"dy": 3}, {"dy": 2}], (0,), (root_y,), (0,)),
        ([{"dz": 3}, {"dz": 5}], (0,), (0, 1, 2, 3), (0,)),
        ([{"dz": 1}, {"dz": 7}], (0,), (0, 1, 2, 3), (0, 3, 5)),
        ([{"dx": 1}, {"dx": 3}, {"dx": 2}], (0,), (0, 1, 2, 3), range(8)),
    )[index]
    parts = []
    for move in moves:
        zs = (0, 3) if move == {"dz": 7} else at_z

        def keep(p, s, zs=zs):
            return p // 2 in at_x and p % 2 in cores and s % 4 in at_y and s // 4 in zs

        parts.append(shifted(value, keep=keep, **move))
    return parts


def scatter_rows(own):
    parts = []
    for i in range(4):
        pairs = []
        for q in range(4):
            for t in range(8):
                row = 8 * q + t // 4 * 4
                pairs.append(((0, 8 * q + t), (t, row + i)))
                pairs.append(((1, 8 * q + t), (t, row + (i + 2) % 4)))
        parts.append(send(own[256 * i : 256 * (i + 1)], pairs))
    return parts


def halve_rows(parts):
    low, high = parts[0] + parts[1], parts[2] + parts[3]
    here = jnp.concatenate([low[:128], high[:128]], axis=0)
    there = jnp.concatenate([low[128:], high[128:]], axis=0)
    pairs = []
    for q in range(ROWS):
        for c in range(0, COLS, 8):
            for y in range(4):
                z = q // 4 * 4
                pairs.append(((q, c + z + y), (q, c + 4 - z + y)))
    return here, send(there, pairs)


def eliminate(block):
    sub = lax.broadcasted_iota(jnp.int32, (8, 128), 0)
    lane = lax.broadcasted_iota(jnp.int32, (8, 128), 1)
    full = lambda x: jnp.broadcast_to(x, (8, 128))
    left = [block[8 * i : 8 * i + 8, :] for i in range(16)]
    right = [jnp.where(lane == sub + 8 * i, 1.0, 0.0) for i in range(16)]
    upper, inverse = [], []
    for b in range(16):
        c = 8 * b
        rows = left[b]
        cols = [full(rows[:, c + k : c + k + 1]) for k in range(8)]
        e = [[full(cols[k][i : i + 1, :]) if i >= k else None for k in range(8)] for i in range(8)]
        rec = []
        low = [[None] * 8 for _ in range(8)]
        for j in range(8):
            rec.append(1.0 / e[j][j])
            for i in range(j + 1, 8):
                low[i][j] = e[i][j] * rec[j]
            for i in range(j + 1, 8):
                for k in range(j + 1, i + 1):
                    e[i][k] = e[i][k] - low[i][j] * e[k][j]
        n = [[None] * 8 for _ in range(8)]
        for j in range(8):
            for i in range(j + 1, 8):
                t = low[i][j]
                for k in range(j + 1, i):
                    t = t + low[i][k] * n[k][j]
                n[i][j] = -t
        scale = [lax.rsqrt(e[j][j]) for j in range(8)]
        s = [[None] * 8 for _ in range(8)]
        for i in range(8):
            for j in range(i + 1):
                t = rec[i] * n[i][j] if j < i else rec[i]
                for k in range(i + 1, 8):
                    t = t + (n[k][i] * rec[k]) * n[k][j]
                s[i][j] = t
                s[j][i] = t
        row_left = [full(rows[k : k + 1, :]) for k in range(8)]
        row_right = [full(right[b][k : k + 1, :]) for k in range(8)]
        def stack(parts):
            v = parts[0]
            for i in range(1, 8):
                if parts[i] is not None:
                    v = jnp.where(sub == i, parts[i], v if v is not None else 0.0)
            return v if v is not None else None
        gl = gr = ul = ur = None
        for k in range(8):
            sc = stack([s[i][k] for i in range(8)])
            col = jnp.where(sub == k, scale[k], 0.0)
            for i in range(k + 1, 8):
                col = jnp.where(sub == i, n[i][k] * scale[i], col)
            a1, a2, a3, a4 = sc * row_left[k], sc * row_right[k], col * row_left[k], col * row_right[k]
            gl = a1 if gl is None else gl + a1
            gr = a2 if gr is None else gr + a2
            ul = a3 if ul is None else ul + a3
            ur = a4 if ur is None else ur + a4
        upper.append(jnp.where(lane >= sub + c, ul, 0.0))
        inverse.append(ur)
        gl_rows = [full(gl[k : k + 1, :]) for k in range(8)]
        gr_rows = [full(gr[k : k + 1, :]) for k in range(8)]
        for i in range(b + 1, 16):
            tl = tr = None
            for k in range(8):
                f = full(left[i][:, c + k : c + k + 1])
                x, y = f * gl_rows[k], f * gr_rows[k]
                tl = x if tl is None else tl + x
                tr = y if tr is None else tr + y
            left[i] = left[i] - tl
            right[i] = right[i] - tr
    return jnp.concatenate(upper, 0), jnp.concatenate(inverse, 0)


def factor_part(work, upper, inverse):
    upper[128:256, 0:128] = jnp.zeros((128, 128), jnp.float32)
    inverse[0:128, 128:256] = jnp.zeros((128, 128), jnp.float32)

    @pl.loop(0, 2)
    def _(k):
        here = pl.ds(pl.multiple_of(128 * k, 128), 128)
        up, inv = eliminate(work[here, here])
        upper[here, here] = up
        inverse[here, here] = inv

        @pl.when(k == 0)
        def _():
            right = dot(inv, work[0:128, 128:256])
            upper[0:128, 128:256] = right
            work[128:256, 128:256] -= dot(right, right, ((0,), (0,)))

    down = dot(upper[0:128, 128:256], inverse[0:128, 0:128], ((0,), (0,)))
    inverse[128:256, 0:128] = -dot(inverse[128:256, 128:256], down)


def factor_first_kernel(mine, other, upper, inverse, work):
    for h in range(2):
        rows = pl.ds(h, 128, stride=2)
        work[0:128, 128 * h : 128 * h + 128] = mine[rows, :] + other[rows, :]
    work[128:256, 128:256] = mine[256:384, :] + other[256:384, :]
    factor_part(work, upper, inverse)


def factor_second_kernel(place, mine, other, upper0, inverse0, upper, inverse, work, up, inv):
    odd = place[0] % 2 == 1
    side = up
    for h in range(2):
        lanes = slice(128 * h, 128 * h + 128)
        here, there = mine[pl.ds(h, 256, stride=2), :], other[pl.ds(h, 256, stride=2), :]
        side[:, lanes] = jnp.where(odd, there, here)
        work[:, lanes] = jnp.where(odd, here, there)
    right = dot(inverse0[...], side[...])
    work[...] -= dot(right, right, ((0,), (0,)))
    factor_part(work, up, inv)
    zero = jnp.zeros((256, 256), jnp.float32)
    upper[0] = upper0[...]
    upper[1] = up[...]
    inverse[0:256, 0:256] = inverse0[...]
    inverse[0:256, 256:512] = zero
    inverse[256:512, 256:512] = inv[...]
    inverse[256:512, 0:256] = -dot(inv[...], dot(right, inverse0[...], ((0,), (0,))))


VMEM = pl.BlockSpec(memory_space=pltpu.VMEM)
SMEM = pl.BlockSpec(memory_space=pltpu.SMEM)


def factor_first(mine, other):
    block = jax.ShapeDtypeStruct((256, 256), jnp.float32)
    return pl.pallas_call(
        factor_first_kernel,
        out_shape=(block, block),
        in_specs=[VMEM, VMEM],
        out_specs=(VMEM, VMEM),
        scratch_shapes=[pltpu.VMEM((256, 256), jnp.float32)],
        compiler_params=pltpu.CompilerParams(vmem_limit_bytes=16 << 20),
        cost_estimate=pl.CostEstimate(flops=60_000_000_000, bytes_accessed=1 << 20, transcendentals=0),
        name="factor_first",
    )(mine, other)


def factor_second(place, mine, other, upper, inverse):
    return pl.pallas_call(
        factor_second_kernel,
        out_shape=(
            jax.ShapeDtypeStruct((2, 256, 256), jnp.float32),
            jax.ShapeDtypeStruct((512, 512), jnp.float32),
        ),
        in_specs=[SMEM, VMEM, VMEM, VMEM, VMEM],
        out_specs=(VMEM, VMEM),
        scratch_shapes=[pltpu.VMEM((256, 256), jnp.float32) for _ in range(3)],
        compiler_params=pltpu.CompilerParams(vmem_limit_bytes=16 << 20),
        cost_estimate=pl.CostEstimate(flops=60_000_000_000, bytes_accessed=1 << 20, transcendentals=0),
        name="factor_second",
    )(place, mine, other, upper, inverse)


FAR_Z = (0, 1, 7, 2, 6, 3, 5, 4)
FAR_Y = (0, 1, 3, 2)


def split(value):
    high = value.astype(jnp.bfloat16)
    return high, (value - high.astype(jnp.float32)).astype(jnp.bfloat16)


def update_kernel(place, a, *refs):
    parts, (mine, other, upper, inverse, out, weight, high, low, w_high, w_low) = refs[:9], refs[9:]
    r = pl.program_id(0)
    p, s = place[0], place[1]

    @pl.when(r == 0)
    def _():
        for g in range(8):
            zz = (s // 4 + 8 - FAR_Z[g]) % 8
            q, late = zz // 2, jnp.where(zz % 2 == p // 4, 0, 32)
            for u in range(4):
                yy = (s % 4 + 4 - FAR_Y[u]) % 4
                part, first = (parts[g], 256 * u) if g < 7 else (parts[7 + u // 2], 256 * (u % 2))
                for slot in range(2):
                    if slot == 0:
                        k = jnp.where(yy < 2, 64 * yy, 128 + 64 * yy) + late
                    else:
                        k = jnp.where(yy < 2, 384 + 64 * yy, 64 * yy) + late
                    rows = pl.ds(pl.multiple_of(q * 512 + k, 32), 32)
                    for ch in range(4):
                        lanes = slice(128 * ch, 128 * ch + 128)
                        value = part[pl.ds(first + 128 * slot + ch, 32, stride=4), :]
                        high[rows, lanes], low[rows, lanes] = split(value)
        odd = p % 2 == 1
        for ch in range(4):
            lanes = slice(128 * ch, 128 * ch + 128)
            here, there = mine[pl.ds(ch, 256, stride=4), :], other[pl.ds(ch, 256, stride=4), :]
            weight[0:256, lanes] = jnp.where(odd, there, here)
            weight[256:512, lanes] = jnp.where(odd, here, there)
        half = dot(inverse[...], weight[...])
        row = lax.broadcasted_iota(jnp.int32, (512, 512), 0)
        col = lax.broadcasted_iota(jnp.int32, (512, 512), 1)
        pick = jnp.where(row == col + 256 * s, -1.0, 0.0)
        half = jnp.where((col < 256) & (s < 2), pick, half)
        w_high[...], w_low[...] = split(dot(inverse[...], half, ((0,), (0,))))

    c, q = r // 4, r % 4
    block = (pl.ds(pl.multiple_of(q * 512, 512), 512), pl.ds(pl.multiple_of(c * 256, 256), 256))
    x_high, x_low = high[block], low[block]

    def times(x, w):
        return lax.dot_general(x, w, (((0,), (0,)), ((), ())), preferred_element_type=jnp.float32)

    product = times(x_high, w_high[...]) + (times(x_high, w_low[...]) + times(x_low, w_high[...]))
    for ch in range(4):
        kept = a[pl.ds(ch, 256, stride=4), :]
        if ch < 2:
            kept = jnp.where(s < 2, 0.0, kept)
        out[pl.ds(ch, 256, stride=4), :] = kept - product[:, 128 * ch : 128 * ch + 128]

    @pl.when((r == 0) & (p < 2))
    def _():
        for ch in range(4):
            where = pl.ds(ch, 256, stride=4)
            if ch >= 2:
                out[where, :] = jnp.zeros((256, 128), jnp.float32)
            else:
                diagonal = upper[jnp.minimum(p, 1), 128 * ch : 128 * ch + 128, :].T
                natural = out[where, :]
                out[where, :] = jnp.where(s == p, diagonal, jnp.where(s > p, 0.0, natural))


def update(place, a, parts, mine, other, upper, inverse):
    return pl.pallas_call(
        update_kernel,
        out_shape=jax.ShapeDtypeStruct(a.shape, jnp.float32),
        grid=(8,),
        in_specs=[SMEM, pl.BlockSpec((1024, 128), lambda r: (r, 0))] + [VMEM] * 13,
        out_specs=pl.BlockSpec((1024, 128), lambda r: (r, 0)),
        scratch_shapes=[
            pltpu.VMEM((512, 512), jnp.float32),
            pltpu.VMEM((2048, 512), jnp.bfloat16),
            pltpu.VMEM((2048, 512), jnp.bfloat16),
            pltpu.VMEM((512, 512), jnp.bfloat16),
            pltpu.VMEM((512, 512), jnp.bfloat16),
        ],
        compiler_params=pltpu.CompilerParams(vmem_limit_bytes=40 << 20),
        cost_estimate=pl.CostEstimate(flops=8_000_000_000, bytes_accessed=16 << 20, transcendentals=0),
        name="update",
    )(place, a, *parts, mine, other, upper, inverse)


def per_device(kernel):
    p, s = lax.axis_index("prow"), lax.axis_index("pcol")
    place = jnp.stack([p, s]).astype(jnp.int32)
    a = kernel.reshape(8192, 128)
    own = a[:1024]
    block = own.reshape(256, 4, 128)[:, :2]

    rows = scatter_rows(own)

    first = jnp.concatenate([block[:128].reshape(256, 128), block[128:, 1]], axis=0)
    first = jnp.where((p == 0) & (s == 0), first, sum(stage(first, 0, (0,))))
    second = together(block.reshape(512, 128), first)[0]
    second = jnp.where((p < 2) & (s == 1), second, sum(stage(second, 0, (0, 1), 1)))
    first = first + sum(stage(first, 1, (0,)))
    first = first + sum(stage(first, 2, (0,)))
    here, moved = halve_rows(rows)
    near = jnp.where(p // 4 == s // 4 % 2, here, moved)
    near = together(near, first)[0]
    column = [near] + [shifted(near, dy=k) for k in (1, 3, 2)]
    column = jnp.concatenate(column, axis=0)
    second = second + sum(stage(second, 1))
    parts = stage(first, 3, (0,))
    column, second, first = together(column, second, first)

    up1, down1 = shifted(column, dz=1), shifted(column, dz=7)
    first = first + sum(parts)
    first_other = send(first, [((q, c), (q + 1, c)) for q in range(0, ROWS, 2) for c in range(COLS)])
    parts = stage(second, 2)
    up1, down1, first, first_other, second, *parts = together(
        up1, down1, first, first_other, second, *parts
    )

    second = second + sum(parts)
    parts = stage(second, 3)
    up2, down2 = shifted(up1, dz=1), shifted(down1, dz=7)
    upper, inverse = factor_first(first, first_other)
    up2, down2, second, upper, inverse, *parts = together(
        up2, down2, second, upper, inverse, *parts
    )

    second = second + sum(parts)
    second_other = swap_cores(second)
    mine = stage(together(own, upper)[0], 3)
    up3, down3 = shifted(up2, dz=1), shifted(down2, dz=7)
    upper, inverse = factor_second(place, second, second_other, upper, inverse)
    up3, down3, upper, inverse = together(up3, down3, upper, inverse)

    up4, down4 = shifted(up3[:512], dz=1), shifted(down3[512:], dz=7)
    up4, down4, *mine = together(up4, down4, *mine)
    mine = jnp.where(p < 2, own, sum(mine))
    other = swap_cores(mine)
    parts = [column, up1, down1, up2, down2, up3, down3, up4, down4]
    out = update(place, a, parts, mine, other, upper, inverse)
    return out.reshape(kernel.shape)


def solution(mesh):
    spec = P(None, "prow", None, None, "pcol", None)
    return jax.shard_map(per_device, mesh=mesh, in_specs=(spec,), out_specs=spec, check_vma=False)
```

time: 198 us -> 134 us (0.68)
  starting transfers between devices: 94.2 us -> 64.2 us
  Pallas kernels: 60.2 us -> 34.8 us
  between operations: 14 us -> 0.73 us
  waiting for transfers between devices: 19.2 us -> 29.1 us
  other arithmetic: 2.92 us -> 0.63 us
  local copies, waits for them, and re-layouts: 5.98 us -> 3.8 us
    ppermute x42, starting transfers between devices: 94.2 us -> 64.2 us  [send(): return lax.ppermute(value, AXES, flat)]
    pallas_call x1 -> x2, Pallas kernels: 46.3 us -> 23.4 us  [the longest x1 12.9 us: factor_second(): pl.pallas_call(factor_second_kernel, out_shape=(jax.ShapeDtypeStruct((2,...]
    ppermute x42, waiting for transfers between devices: 19.1 us -> 29.1 us  [send(): return lax.ppermute(value, AXES, flat)]
    unnamed x4, local copies, waits for them, and re-layouts: 4.37 us -> 0.59 us
    pallas_call x1, Pallas kernels: 13.9 us -> 11.4 us  [update(): pl.pallas_call(update_kernel, out_shape=jax.ShapeDtypeStruct(a.shape, jnp...]
  transfers between devices with their start and end apart: 43 -> 42, of which waited for: 10 -> 11; matrix products, arithmetic and copies ran while one was open for 1% -> 2% of each run, Pallas kernels for 24% -> 18%
where the time goes in v2:
time: 134 us; the launch traced here: 133 us
  starting transfers between devices  64.2 us (48%)
  Pallas kernels  34.8 us (26%)
  waiting for transfers between devices  29.1 us (22%)
  local copies, waits for them, and re-layouts  3.8 us (3%)
    ppermute x42, starting transfers between devices, send(): return lax.ppermute(value, AXES, flat)  64.2 us
    ppermute x42, waiting for transfers between devices, send(): return lax.ppermute(value, AXES, flat)  29.1 us
    pallas_call x1, Pallas kernels, factor_second(): pl.pallas_call(factor_second_kernel, out_shape=(jax.ShapeDtypeStruct((2,...  12.9 us
    pallas_call x1, Pallas kernels, update(): pl.pallas_call(update_kernel, out_shape=jax.ShapeDtypeStruct(a.shape, jnp...  11.4 us
    pallas_call x1, Pallas kernels, factor_first(): pl.pallas_call(factor_first_kernel, out_shape=(block, block), in_specs=[V...  10.5 us
  transfers between devices with their start and end apart: 42, of which 11 were waited for; matrix products, arithmetic and copies ran while one was open for 2% of the time, Pallas kernels for 18%

profile of v2, /device:TPU:1, one launch (start us, length us, event | category | flops | bytes accessed | tf_op | source)
XLA Modules:
  0.0 133.3 jit_solution(14827805384392979641)
XLA Ops:
  0.0 1.5 %fusion = (f32[1,1,64,2,1,256]{5,4,3,2,1,0:T(1,128)S(1)}, f32[1,1,64,2,1,256]{5,4,3,2,1,0:T(1,128)S(1)}, f32[1,1,64,2,1,256]{5,4,3,2,1,0:T(1,128)S(1)}, f32[1,1,64,2,1,256]{5,4,3,2,1,0:T(1,128)S(1)}) fusion(f32[8,1,256,2,1,256]{5,4,3,2,1,0:T(1,128)} %param.1), kind=kLoop, calls=%fused_computation.14 | loop fusion | bytes 1048576 | tf_op jit(solution)/shard_map/slice | solution.py:75
  1.5 6.0 %collective-permute-start.1 = (f32[256,128]{1,0:T(8,128)S(1)}, f32[256,128]{1,0:T(8,128)S(1)}, u32[]{:S(2)}, u32[]{:S(2)}) collective-permute-start(f32[256,128]{1,0:T(8,128)S(1)} %bitcast.32), channel_id=1, source_target_pairs={{0,1},{32,3},{1,33},{33,35},{2,65},{34,67},{3,97},{35,99},{4,133},... | collective-permute-start | bytes 393224 | tf_op jit(solution)/shard_map/ppermute | solution.py:21
  7.5 3.5 %collective-permute-start = (f32[256,128]{1,0:T(8,128)S(1)}, f32[256,128]{1,0:T(8,128)S(1)}, u32[]{:S(2)}, u32[]{:S(2)}) collective-permute-start(f32[256,128]{1,0:T(8,128)S(1)} %bitcast.31), channel_id=1, source_target_pairs={{0,0},{32,2},{1,32},{33,34},{2,64},{34,66},{3,96},{35,98},{4,132},... | collective-permute-start | bytes 393224 | tf_op jit(solution)/shard_map/ppermute | solution.py:21
  11.0 1.9 %collective-permute-start.2 = (f32[256,128]{1,0:T(8,128)S(1)}, f32[256,128]{1,0:T(8,128)S(1)}, u32[]{:S(2)}, u32[]{:S(2)}) collective-permute-start(f32[256,128]{1,0:T(8,128)S(1)} %bitcast.30), channel_id=1, source_target_pairs={{0,2},{32,0},{1,34},{33,32},{2,66},{34,64},{3,98},{35,96},{4,134},... | collective-permute-start | bytes 393224 | tf_op jit(solution)/shard_map/ppermute | solution.py:21
  12.9 2.4 %collective-permute-start.3 = (f32[256,128]{1,0:T(8,128)S(1)}, f32[256,128]{1,0:T(8,128)S(1)}, u32[]{:S(2)}, u32[]{:S(2)}) collective-permute-start(f32[256,128]{1,0:T(8,128)S(1)} %bitcast.29), channel_id=1, source_target_pairs={{0,3},{32,1},{1,35},{33,33},{2,67},{34,65},{3,99},{35,97},{4,135},... | collective-permute-start | bytes 393224 | tf_op jit(solution)/shard_map/ppermute | solution.py:21
  15.3 1.4 %slice.75 = f32[1,1,256,2,1,256]{5,4,3,2,1,0:T(1,128)S(1)} slice(f32[8,1,256,2,1,256]{5,4,3,2,1,0:T(1,128)} %param.1), slice={[0:1], [0:1], [0:256], [0:2], [0:1], [0:256]} | slice | bytes 1048576 | tf_op jit(solution)/shard_map/slice | solution.py:342
  24.1 4.0 %collective-permute-start.4 = (f32[256,128]{1,0:T(8,128)S(1)}, f32[256,128]{1,0:T(8,128)S(1)}, u32[]{:S(2)}, u32[]{:S(2)}) collective-permute-start(f32[256,128]{1,0:T(8,128)S(1)} %pad_maximum_fusion.2), channel_id=1, source_target_pairs={{0,4},{1,5},{2,6},{3,7},{8,12},{9,13},{10,14},{11,15},{16,20},{17,... | collective-permute-start | bytes 393224 | tf_op jit(solution)/shard_map/ppermute | solution.py:21
  29.5 1.6 %collective-permute-done.16 = f32[512,128]{1,0:T(8,128)S(1)} collective-permute-done((f32[512,128]{1,0:T(8,128)S(1)}, f32[512,128]{1,0:T(8,128)S(1)}, u32[]{:S(2)}, u32[]{:S(2)}) %collective-permute-start.16) | collective-permute-done | bytes 262176 | tf_op jit(solution)/shard_map/ppermute | solution.py:21
  31.2 4.6 %collective-permute-start.19 = (f32[512,128]{1,0:T(8,128)S(1)}, f32[512,128]{1,0:T(8,128)S(1)}, u32[]{:S(2)}, u32[]{:S(2)}) collective-permute-start(f32[512,128]{1,0:T(8,128)S(1)} %add_select_fusion.1), channel_id=1, source_target_pairs={{0,20},{1,21},{2,22},{3,23},{32,52},{33,53},{34,54},{35,55}} | collective-permute-start | bytes 786440 | tf_op jit(solution)/shard_map/ppermute | solution.py:21
  35.8 1.3 collective-permute-start.18
  38.5 1.4 %collective-permute-start.14 = (f32[256,128]{1,0:T(8,128)S(1)}, f32[256,128]{1,0:T(8,128)S(1)}, u32[]{:S(2)}, u32[]{:S(2)}) collective-permute-start(f32[256,128]{1,0:T(8,128)S(1)} %maximum_select_fusion), channel_id=1, source_target_pairs={{0,2},{1,3},{2,0},{3,1},{4,6},{5,7},{6,4},{7,5},{8,10},{9,11},{10,... | collective-permute-start | bytes 393224 | tf_op jit(solution)/shard_map/ppermute | solution.py:21
  41.2 1.3 collective-permute-done.18
  45.0 2.5 %collective-permute-done.12 = f32[256,128]{1,0:T(8,128)S(1)} collective-permute-done((f32[256,128]{1,0:T(8,128)S(1)}, f32[256,128]{1,0:T(8,128)S(1)}, u32[]{:S(2)}, u32[]{:S(2)}) %collective-permute-start.12) | collective-permute-done | bytes 131104 | tf_op jit(solution)/shard_map/ppermute | solution.py:21
  47.6 1.5 %collective-permute-start.20 = (f32[1024,128]{1,0:T(8,128)S(1)}, f32[1024,128]{1,0:T(8,128)S(1)}, u32[]{:S(2)}, u32[]{:S(2)}) collective-permute-start(f32[1024,128]{1,0:T(8,128)S(1)} %pad_maximum_fusion.refs_0_), channel_id=1, source_target_pairs={{0,4},{1,5},{2,6},{3,7},{4,8},{5,9},{6,10},{7,11},{8,12},{9,13},{1... | collective-permute-start | bytes 1572872 | tf_op jit(solution)/shard_map/ppermute | solution.py:21
  49.1 3.2 %collective-permute-start.27 = (f32[512,128]{1,0:T(8,128)S(1)}, f32[512,128]{1,0:T(8,128)S(1)}, u32[]{:S(2)}, u32[]{:S(2)}) collective-permute-start(f32[512,128]{1,0:T(8,128)S(1)} %add_add_fusion.2), channel_id=1, source_target_pairs={{0,28},{1,29},{2,30},{3,31},{12,8},{13,9},{14,10},{15,11},{32,60},... | collective-permute-start | bytes 786440 | tf_op jit(solution)/shard_map/ppermute | solution.py:21
  52.3 1.3 collective-permute-start.26
  55.0 12.7 %collective-permute-done.25.other = f32[384,128]{1,0:T(8,128)S(1)} collective-permute-done((f32[384,128]{1,0:T(8,128)S(1)}, f32[384,128]{1,0:T(8,128)S(1)}, u32[]{:S(2)}, u32[]{:S(2)}) %collective-permute-start.25) | collective-permute-done | bytes 196640 | tf_op jit(solution)/shard_map/ppermute | solution.py:21
  67.7 1.3 collective-permute-start.32
  71.7 2.7 %collective-permute-start.29 = (f32[1024,128]{1,0:T(8,128)S(1)}, f32[1024,128]{1,0:T(8,128)S(1)}, u32[]{:S(2)}, u32[]{:S(2)}) collective-permute-start(f32[1024,128]{1,0:T(8,128)S(1)} %collective-permute-done.21.refs_2_), channel_id=1, source_target_pairs={{0,28},{1,29},{2,30},{3,31},{4,0},{5,1},{6,2},{7,3},{8,4},{9,5},{1... | collective-permute-start | bytes 1572872 | tf_op jit(solution)/shard_map/ppermute | solution.py:21
  74.4 10.5 %factor_first.1 = (f32[256,256]{1,0:T(8,128)S(1)}, f32[256,256]{1,0:T(8,128)S(1)}) custom-call(f32[384,128]{1,0:T(8,128)S(1)} %add_add_fusion.3.mine, f32[384,128]{1,0:T(8,128)S(1)} %collective-permute-done.25.other), custom_call_target="tpu_custom_call" | custom-call | flops 60000002048 | bytes 1048576 | tf_op jit(solution)/shard_map/factor_first/pallas_call | solution.py:219
  85.0 3.3 %collective-permute-start.35 = (f32[512,128]{1,0:T(8,128)S(1)}, f32[512,128]{1,0:T(8,128)S(1)}, u32[]{:S(2)}, u32[]{:S(2)}) collective-permute-start(f32[512,128]{1,0:T(8,128)S(1)} %add_add_fusion.mine), channel_id=1, source_target_pairs={{0,32},{1,33},{2,34},{3,35},{4,36},{5,37},{6,38},{7,39},{8,40},{9,... | collective-permute-start | bytes 786440 | tf_op jit(solution)/shard_map/ppermute | solution.py:21
  88.4 1.6 %collective-permute-start.40 = (f32[1024,128]{1,0:T(8,128)S(1)}, f32[1024,128]{1,0:T(8,128)S(1)}, u32[]{:S(2)}, u32[]{:S(2)}) collective-permute-start(f32[1024,128]{1,0:T(8,128)S(1)} %bitcast.14), channel_id=1, source_target_pairs={{0,128},{1,129},{2,130},{3,131},{4,132},{5,133},{6,134},{7,135},{8... | collective-permute-start | bytes 1572872 | tf_op jit(solution)/shard_map/ppermute | solution.py:21
  90.0 1.3 collective-permute-start.39
  91.3 1.3 collective-permute-start.38
  93.7 1.7 %collective-permute-start.34 = (f32[1024,128]{1,0:T(8,128)S(1)}, f32[1024,128]{1,0:T(8,128)S(1)}, u32[]{:S(2)}, u32[]{:S(2)}) collective-permute-start(f32[1024,128]{1,0:T(8,128)S(1)} %collective-permute-done.29.refs_4_), channel_id=1, source_target_pairs={{0,28},{1,29},{2,30},{3,31},{4,0},{5,1},{6,2},{7,3},{8,4},{9,5},{1... | collective-permute-start | bytes 1572872 | tf_op jit(solution)/shard_map/ppermute | solution.py:21
  95.4 12.9 %factor_second.1 = (f32[2,256,256]{2,1,0:T(8,128)S(1)}, f32[512,512]{1,0:T(8,128)S(1)}) custom-call(s32[2]{0:T(128)S(1)} %pad_add_fusion.place, f32[512,128]{1,0:T(8,128)S(1)} %add_add_fusion.mine, f32[512,128]{1,0:T(8,128)S(1)} %collective-permute-done.35.other, f32[256,256]{1,0:T(8,128)S(1)} %get-tuple-element.59.upper0, ...), custom_call_target="tpu_custom_call" | custom-call | flops 60000002048 | bytes 1048576 | tf_op jit(solution)/shard_map/factor_second/pallas_call | solution.py:232
  108.4 1.6 %collective-permute-start.37 = (f32[512,128]{1,0:T(8,128)S(1)}, f32[512,128]{1,0:T(8,128)S(1)}, u32[]{:S(2)}, u32[]{:S(2)}) collective-permute-start(f32[512,128]{1,0:T(8,128)S(1)} %slice.80), channel_id=1, source_target_pairs={{0,28},{1,29},{2,30},{3,31},{4,0},{5,1},{6,2},{7,3},{8,4},{9,5},{1... | collective-permute-start | bytes 786440 | tf_op jit(solution)/shard_map/ppermute | solution.py:21
  110.9 1.8 %collective-permute-done.38 = f32[1024,128]{1,0:T(8,128)S(1)} collective-permute-done((f32[1024,128]{1,0:T(8,128)S(1)}, f32[1024,128]{1,0:T(8,128)S(1)}, u32[]{:S(2)}, u32[]{:S(2)}) %collective-permute-start.38) | collective-permute-done | bytes 524320 | tf_op jit(solution)/shard_map/ppermute | solution.py:21
  112.7 4.0 %collective-permute-done.37.refs_8_ = f32[512,128]{1,0:T(8,128)S(1)} collective-permute-done((f32[512,128]{1,0:T(8,128)S(1)}, f32[512,128]{1,0:T(8,128)S(1)}, u32[]{:S(2)}, u32[]{:S(2)}) %collective-permute-start.37) | collective-permute-done | bytes 262176 | tf_op jit(solution)/shard_map/ppermute | solution.py:21
  117.7 2.7 %collective-permute-start.41 = (f32[1024,128]{1,0:T(8,128)S(1)}, f32[1024,128]{1,0:T(8,128)S(1)}, u32[]{:S(2)}, u32[]{:S(2)}) collective-permute-start(f32[1024,128]{1,0:T(8,128)S(1)} %add_select_fusion.refs_9_), channel_id=1, source_target_pairs={{0,32},{1,33},{2,34},{3,35},{4,36},{5,37},{6,38},{7,39},{8,40},{9,... | collective-permute-start | bytes 1572872 | tf_op jit(solution)/shard_map/ppermute | solution.py:21
  120.3 1.5 %collective-permute-done.41.refs_10_ = f32[1024,128]{1,0:T(8,128)S(1)} collective-permute-done((f32[1024,128]{1,0:T(8,128)S(1)}, f32[1024,128]{1,0:T(8,128)S(1)}, u32[]{:S(2)}, u32[]{:S(2)}) %collective-permute-start.41) | collective-permute-done | bytes 524320 | tf_op jit(solution)/shard_map/ppermute | solution.py:21
  121.9 11.4 %update.1 = f32[8192,128]{1,0:T(8,128)} custom-call(s32[2]{0:T(128)S(1)} %pad_add_fusion.place, f32[8192,128]{1,0:T(8,128)S(1)} %bitcast.13, f32[1024,128]{1,0:T(8,128)S(1)} %pad_maximum_fusion.refs_0_, f32[1024,128]{1,0:T(8,128)S(1)} %collective-permute-done.20.refs_1_, f32[1024,128]{1,0:T(8,128)S(1)} %collective-permute-done.21.refs_2_, ...), custom_call_target="tpu_custom_call" | custom-call | flops 8000000000 | bytes 16777216 | tf_op jit(solution)/shard_map/update/pallas_call | solution.py:319
  (86 shorter events, 20.9 us)
Async XLA Ops:
  1.5 17.0 %collective-permute-start.1 = (f32[256,128]{1,0:T(8,128)S(1)}, f32[256,128]{1,0:T(8,128)S(1)}, u32[]{:S(2)}, u32[]{:S(2)}) collective-permute-start(f32[256,128]{1,0:T(8,128)S(1)} %bitcast.32), channel_id=1, source_target_pairs={{0,1},{32,3},{1,33},{33,35},{2,65},{34,67},{3,97},{35,99},{4,133},... | collective-permute-start | bytes 393224 | tf_op jit(solution)/shard_map/ppermute | solution.py:21
  7.5 11.7 %collective-permute-start = (f32[256,128]{1,0:T(8,128)S(1)}, f32[256,128]{1,0:T(8,128)S(1)}, u32[]{:S(2)}, u32[]{:S(2)}) collective-permute-start(f32[256,128]{1,0:T(8,128)S(1)} %bitcast.31), channel_id=1, source_target_pairs={{0,0},{32,2},{1,32},{33,34},{2,64},{34,66},{3,96},{35,98},{4,132},... | collective-permute-start | bytes 393224 | tf_op jit(solution)/shard_map/ppermute | solution.py:21
  11.0 8.9 %collective-permute-start.2 = (f32[256,128]{1,0:T(8,128)S(1)}, f32[256,128]{1,0:T(8,128)S(1)}, u32[]{:S(2)}, u32[]{:S(2)}) collective-permute-start(f32[256,128]{1,0:T(8,128)S(1)} %bitcast.30), channel_id=1, source_target_pairs={{0,2},{32,0},{1,34},{33,32},{2,66},{34,64},{3,98},{35,96},{4,134},... | collective-permute-start | bytes 393224 | tf_op jit(solution)/shard_map/ppermute | solution.py:21
  20.7 7.4 %collective-permute-start.8 = (f32[384,128]{1,0:T(8,128)S(1)}, f32[384,128]{1,0:T(8,128)S(1)}, u32[]{:S(2)}, u32[]{:S(2)}) collective-permute-start(f32[384,128]{1,0:T(8,128)S(1)} %add_select_fusion.2), channel_id=1, source_target_pairs={{0,12},{1,13},{2,14},{3,15}} | collective-permute-start | bytes 589832 | tf_op jit(solution)/shard_map/ppermute | solution.py:21
  21.4 7.5 %collective-permute-start.17 = (f32[512,128]{1,0:T(8,128)S(1)}, f32[512,128]{1,0:T(8,128)S(1)}, u32[]{:S(2)}, u32[]{:S(2)}) collective-permute-start(f32[512,128]{1,0:T(8,128)S(1)} %bitcast.23), channel_id=1, source_target_pairs={{1,3},{33,35}} | collective-permute-start | bytes 786440 | tf_op jit(solution)/shard_map/ppermute | solution.py:21
  22.1 9.0 %collective-permute-start.16 = (f32[512,128]{1,0:T(8,128)S(1)}, f32[512,128]{1,0:T(8,128)S(1)}, u32[]{:S(2)}, u32[]{:S(2)}) collective-permute-start(f32[512,128]{1,0:T(8,128)S(1)} %bitcast.24), channel_id=1, source_target_pairs={{1,0},{33,32}} | collective-permute-start | bytes 786440 | tf_op jit(solution)/shard_map/ppermute | solution.py:21
  23.4 7.7 %collective-permute-start.15 = (f32[512,128]{1,0:T(8,128)S(1)}, f32[512,128]{1,0:T(8,128)S(1)}, u32[]{:S(2)}, u32[]{:S(2)}) collective-permute-start(f32[512,128]{1,0:T(8,128)S(1)} %bitcast.25), channel_id=1, source_target_pairs={{1,2},{33,34}} | collective-permute-start | bytes 786440 | tf_op jit(solution)/shard_map/ppermute | solution.py:21
  24.1 13.0 %collective-permute-start.4 = (f32[256,128]{1,0:T(8,128)S(1)}, f32[256,128]{1,0:T(8,128)S(1)}, u32[]{:S(2)}, u32[]{:S(2)}) collective-permute-start(f32[256,128]{1,0:T(8,128)S(1)} %pad_maximum_fusion.2), channel_id=1, source_target_pairs={{0,4},{1,5},{2,6},{3,7},{8,12},{9,13},{10,14},{11,15},{16,20},{17,... | collective-permute-start | bytes 393224 | tf_op jit(solution)/shard_map/ppermute | solution.py:21
  28.2 8.9 %collective-permute-start.11 = (f32[384,128]{1,0:T(8,128)S(1)}, f32[384,128]{1,0:T(8,128)S(1)}, u32[]{:S(2)}, u32[]{:S(2)}) collective-permute-start(f32[384,128]{1,0:T(8,128)S(1)} %add_add_fusion.5), channel_id=1, source_target_pairs={{0,28},{1,29},{2,30},{3,31},{12,8},{13,9},{14,10},{15,11}} | collective-permute-start | bytes 589832 | tf_op jit(solution)/shard_map/ppermute | solution.py:21
  28.9 8.3 %collective-permute-start.10 = (f32[384,128]{1,0:T(8,128)S(1)}, f32[384,128]{1,0:T(8,128)S(1)}, u32[]{:S(2)}, u32[]{:S(2)}) collective-permute-start(f32[384,128]{1,0:T(8,128)S(1)} %add_add_fusion.5), channel_id=1, source_target_pairs={{0,4},{1,5},{2,6},{3,7},{12,16},{13,17},{14,18},{15,19},{20,24},{2... | collective-permute-start | bytes 589832 | tf_op jit(solution)/shard_map/ppermute | solution.py:21
  31.2 10.0 %collective-permute-start.19 = (f32[512,128]{1,0:T(8,128)S(1)}, f32[512,128]{1,0:T(8,128)S(1)}, u32[]{:S(2)}, u32[]{:S(2)}) collective-permute-start(f32[512,128]{1,0:T(8,128)S(1)} %add_select_fusion.1), channel_id=1, source_target_pairs={{0,20},{1,21},{2,22},{3,23},{32,52},{33,53},{34,54},{35,55}} | collective-permute-start | bytes 786440 | tf_op jit(solution)/shard_map/ppermute | solution.py:21
  37.2 11.9 %collective-permute-start.24 = (f32[384,128]{1,0:T(8,128)S(1)}, f32[384,128]{1,0:T(8,128)S(1)}, u32[]{:S(2)}, u32[]{:S(2)}) collective-permute-start(f32[384,128]{1,0:T(8,128)S(1)} %add_add_fusion.4), channel_id=1, source_target_pairs={{0,128},{1,129},{2,130},{3,131},{4,132},{5,133},{6,134},{7,135},{8... | collective-permute-start | bytes 589832 | tf_op jit(solution)/shard_map/ppermute | solution.py:21
  37.9 14.4 %collective-permute-start.23 = (f32[384,128]{1,0:T(8,128)S(1)}, f32[384,128]{1,0:T(8,128)S(1)}, u32[]{:S(2)}, u32[]{:S(2)}) collective-permute-start(f32[384,128]{1,0:T(8,128)S(1)} %add_add_fusion.4), channel_id=1, source_target_pairs={{0,192},{1,193},{2,194},{3,195},{4,196},{5,197},{6,198},{7,199},{8... | collective-permute-start | bytes 589832 | tf_op jit(solution)/shard_map/ppermute | solution.py:21
  43.9 9.7 %collective-permute-start.22 = (f32[384,128]{1,0:T(8,128)S(1)}, f32[384,128]{1,0:T(8,128)S(1)}, u32[]{:S(2)}, u32[]{:S(2)}) collective-permute-start(f32[384,128]{1,0:T(8,128)S(1)} %add_add_fusion.4), channel_id=1, source_target_pairs={{0,64},{1,65},{2,66},{3,67},{4,68},{5,69},{6,70},{7,71},{8,72},{9,... | collective-permute-start | bytes 589832 | tf_op jit(solution)/shard_map/ppermute | solution.py:21
  47.5 20.1 %collective-permute-start.21 = (f32[1024,128]{1,0:T(8,128)S(1)}, f32[1024,128]{1,0:T(8,128)S(1)}, u32[]{:S(2)}, u32[]{:S(2)}) collective-permute-start(f32[1024,128]{1,0:T(8,128)S(1)} %pad_maximum_fusion.refs_0_), channel_id=1, source_target_pairs={{0,28},{1,29},{2,30},{3,31},{4,0},{5,1},{6,2},{7,3},{8,4},{9,5},{1... | collective-permute-start | bytes 1572872 | tf_op jit(solution)/shard_map/ppermute | solution.py:21
  47.6 20.0 %collective-permute-start.20 = (f32[1024,128]{1,0:T(8,128)S(1)}, f32[1024,128]{1,0:T(8,128)S(1)}, u32[]{:S(2)}, u32[]{:S(2)}) collective-permute-start(f32[1024,128]{1,0:T(8,128)S(1)} %pad_maximum_fusion.refs_0_), channel_id=1, source_target_pairs={{0,4},{1,5},{2,6},{3,7},{4,8},{5,9},{6,10},{7,11},{8,12},{9,13},{1... | collective-permute-start | bytes 1572872 | tf_op jit(solution)/shard_map/ppermute | solution.py:21
  49.1 18.6 %collective-permute-start.27 = (f32[512,128]{1,0:T(8,128)S(1)}, f32[512,128]{1,0:T(8,128)S(1)}, u32[]{:S(2)}, u32[]{:S(2)}) collective-permute-start(f32[512,128]{1,0:T(8,128)S(1)} %add_add_fusion.2), channel_id=1, source_target_pairs={{0,28},{1,29},{2,30},{3,31},{12,8},{13,9},{14,10},{15,11},{32,60},... | collective-permute-start | bytes 786440 | tf_op jit(solution)/shard_map/ppermute | solution.py:21
  52.3 15.3 %collective-permute-start.26 = (f32[512,128]{1,0:T(8,128)S(1)}, f32[512,128]{1,0:T(8,128)S(1)}, u32[]{:S(2)}, u32[]{:S(2)}) collective-permute-start(f32[512,128]{1,0:T(8,128)S(1)} %add_add_fusion.2), channel_id=1, source_target_pairs={{0,4},{1,5},{2,6},{3,7},{12,16},{13,17},{14,18},{15,19},{20,24},{2... | collective-permute-start | bytes 786440 | tf_op jit(solution)/shard_map/ppermute | solution.py:21
  53.7 14.0 %collective-permute-start.25 = (f32[384,128]{1,0:T(8,128)S(1)}, f32[384,128]{1,0:T(8,128)S(1)}, u32[]{:S(2)}, u32[]{:S(2)}) collective-permute-start(f32[384,128]{1,0:T(8,128)S(1)} %add_add_fusion.3.mine), channel_id=1, source_target_pairs={{0,32},{1,33},{2,34},{3,35},{4,36},{5,37},{6,38},{7,39},{8,40},{9,... | collective-permute-start | bytes 589832 | tf_op jit(solution)/shard_map/ppermute | solution.py:21
  67.7 17.2 %collective-permute-start.32 = (f32[512,128]{1,0:T(8,128)S(1)}, f32[512,128]{1,0:T(8,128)S(1)}, u32[]{:S(2)}, u32[]{:S(2)}) collective-permute-start(f32[512,128]{1,0:T(8,128)S(1)} %add_add_fusion.1), channel_id=1, source_target_pairs={{0,128},{1,129},{2,130},{3,131},{4,132},{5,133},{6,134},{7,135},{8... | collective-permute-start | bytes 786440 | tf_op jit(solution)/shard_map/ppermute | solution.py:21
  69.0 15.9 %collective-permute-start.31 = (f32[512,128]{1,0:T(8,128)S(1)}, f32[512,128]{1,0:T(8,128)S(1)}, u32[]{:S(2)}, u32[]{:S(2)}) collective-permute-start(f32[512,128]{1,0:T(8,128)S(1)} %add_add_fusion.1), channel_id=1, source_target_pairs={{0,192},{1,193},{2,194},{3,195},{4,196},{5,197},{6,198},{7,199},{8... | collective-permute-start | bytes 786440 | tf_op jit(solution)/shard_map/ppermute | solution.py:21
  70.3 14.6 %collective-permute-start.30 = (f32[512,128]{1,0:T(8,128)S(1)}, f32[512,128]{1,0:T(8,128)S(1)}, u32[]{:S(2)}, u32[]{:S(2)}) collective-permute-start(f32[512,128]{1,0:T(8,128)S(1)} %add_add_fusion.1), channel_id=1, source_target_pairs={{0,64},{1,65},{2,66},{3,67},{4,68},{5,69},{6,70},{7,71},{8,72},{9,... | collective-permute-start | bytes 786440 | tf_op jit(solution)/shard_map/ppermute | solution.py:21
  71.7 13.3 %collective-permute-start.28 = (f32[1024,128]{1,0:T(8,128)S(1)}, f32[1024,128]{1,0:T(8,128)S(1)}, u32[]{:S(2)}, u32[]{:S(2)}) collective-permute-start(f32[1024,128]{1,0:T(8,128)S(1)} %collective-permute-done.20.refs_1_), channel_id=1, source_target_pairs={{0,4},{1,5},{2,6},{3,7},{4,8},{5,9},{6,10},{7,11},{8,12},{9,13},{1... | collective-permute-start | bytes 1572872 | tf_op jit(solution)/shard_map/ppermute | solution.py:21
  71.7 13.2 %collective-permute-start.29 = (f32[1024,128]{1,0:T(8,128)S(1)}, f32[1024,128]{1,0:T(8,128)S(1)}, u32[]{:S(2)}, u32[]{:S(2)}) collective-permute-start(f32[1024,128]{1,0:T(8,128)S(1)} %collective-permute-done.21.refs_2_), channel_id=1, source_target_pairs={{0,28},{1,29},{2,30},{3,31},{4,0},{5,1},{6,2},{7,3},{8,4},{9,5},{1... | collective-permute-start | bytes 1572872 | tf_op jit(solution)/shard_map/ppermute | solution.py:21
  85.0 8.7 %collective-permute-start.35 = (f32[512,128]{1,0:T(8,128)S(1)}, f32[512,128]{1,0:T(8,128)S(1)}, u32[]{:S(2)}, u32[]{:S(2)}) collective-permute-start(f32[512,128]{1,0:T(8,128)S(1)} %add_add_fusion.mine), channel_id=1, source_target_pairs={{0,32},{1,33},{2,34},{3,35},{4,36},{5,37},{6,38},{7,39},{8,40},{9,... | collective-permute-start | bytes 786440 | tf_op jit(solution)/shard_map/ppermute | solution.py:21
  88.4 22.5 %collective-permute-start.40 = (f32[1024,128]{1,0:T(8,128)S(1)}, f32[1024,128]{1,0:T(8,128)S(1)}, u32[]{:S(2)}, u32[]{:S(2)}) collective-permute-start(f32[1024,128]{1,0:T(8,128)S(1)} %bitcast.14), channel_id=1, source_target_pairs={{0,128},{1,129},{2,130},{3,131},{4,132},{5,133},{6,134},{7,135},{8... | collective-permute-start | bytes 1572872 | tf_op jit(solution)/shard_map/ppermute | solution.py:21
  90.0 21.0 %collective-permute-start.39 = (f32[1024,128]{1,0:T(8,128)S(1)}, f32[1024,128]{1,0:T(8,128)S(1)}, u32[]{:S(2)}, u32[]{:S(2)}) collective-permute-start(f32[1024,128]{1,0:T(8,128)S(1)} %bitcast.15), channel_id=1, source_target_pairs={{0,192},{1,193},{2,194},{3,195},{4,196},{5,197},{6,198},{7,199},{8... | collective-permute-start | bytes 1572872 | tf_op jit(solution)/shard_map/ppermute | solution.py:21
  91.3 21.4 %collective-permute-start.38 = (f32[1024,128]{1,0:T(8,128)S(1)}, f32[1024,128]{1,0:T(8,128)S(1)}, u32[]{:S(2)}, u32[]{:S(2)}) collective-permute-start(f32[1024,128]{1,0:T(8,128)S(1)} %bitcast.16), channel_id=1, source_target_pairs={{0,64},{1,65},{2,66},{3,67},{4,68},{5,69},{6,70},{7,71},{8,72},{9,... | collective-permute-start | bytes 1572872 | tf_op jit(solution)/shard_map/ppermute | solution.py:21
  92.6 15.7 %collective-permute-start.33 = (f32[1024,128]{1,0:T(8,128)S(1)}, f32[1024,128]{1,0:T(8,128)S(1)}, u32[]{:S(2)}, u32[]{:S(2)}) collective-permute-start(f32[1024,128]{1,0:T(8,128)S(1)} %collective-permute-done.28.refs_3_), channel_id=1, source_target_pairs={{0,4},{1,5},{2,6},{3,7},{4,8},{5,9},{6,10},{7,11},{8,12},{9,13},{1... | collective-permute-start | bytes 1572872 | tf_op jit(solution)/shard_map/ppermute | solution.py:21
  93.7 14.6 %collective-permute-start.34 = (f32[1024,128]{1,0:T(8,128)S(1)}, f32[1024,128]{1,0:T(8,128)S(1)}, u32[]{:S(2)}, u32[]{:S(2)}) collective-permute-start(f32[1024,128]{1,0:T(8,128)S(1)} %collective-permute-done.29.refs_4_), channel_id=1, source_target_pairs={{0,28},{1,29},{2,30},{3,31},{4,0},{5,1},{6,2},{7,3},{8,4},{9,5},{1... | collective-permute-start | bytes 1572872 | tf_op jit(solution)/shard_map/ppermute | solution.py:21
  108.4 8.4 %collective-permute-start.37 = (f32[512,128]{1,0:T(8,128)S(1)}, f32[512,128]{1,0:T(8,128)S(1)}, u32[]{:S(2)}, u32[]{:S(2)}) collective-permute-start(f32[512,128]{1,0:T(8,128)S(1)} %slice.80), channel_id=1, source_target_pairs={{0,28},{1,29},{2,30},{3,31},{4,0},{5,1},{6,2},{7,3},{8,4},{9,5},{1... | collective-permute-start | bytes 786440 | tf_op jit(solution)/shard_map/ppermute | solution.py:21
  110.0 7.6 %collective-permute-start.36 = (f32[512,128]{1,0:T(8,128)S(1)}, f32[512,128]{1,0:T(8,128)S(1)}, u32[]{:S(2)}, u32[]{:S(2)}) collective-permute-start(f32[512,128]{1,0:T(8,128)S(1)} %slice.79), channel_id=1, source_target_pairs={{0,4},{1,5},{2,6},{3,7},{4,8},{5,9},{6,10},{7,11},{8,12},{9,13},{1... | collective-permute-start | bytes 786440 | tf_op jit(solution)/shard_map/ppermute | solution.py:21
  (11 other events, 74.4 us)

commit v3 on v2

--- a/solution.py
+++ b/solution.py
@@ -253,29 +253,59 @@
     return high, (value - high.astype(jnp.float32)).astype(jnp.bfloat16)
 
 
-def update_kernel(place, a, *refs):
-    parts, (mine, other, upper, inverse, out, weight, high, low, w_high, w_low) = refs[:9], refs[9:]
+def place_part(place, g, part_of, high, low, base):
+    p, s = place[0], place[1]
+    zz = (s // 4 + 8 - FAR_Z[g]) % 8
+    q, late = zz // 2, jnp.where(zz % 2 == p // 4, 0, 32)
+    for u in range(4):
+        yy = (s % 4 + 4 - FAR_Y[u]) % 4
+        part, first = part_of(u)
+        for slot in range(2):
+            if slot == 0:
+                k = jnp.where(yy < 2, 64 * yy, 128 + 64 * yy) + late
+            else:
+                k = jnp.where(yy < 2, 384 + 64 * yy, 64 * yy) + late
+            rows = pl.ds(pl.multiple_of(base * q * 512 + k, 32), 32)
+            for ch in range(4):
+                lanes = slice(128 * ch, 128 * ch + 128)
+                value = part[pl.ds(first + 128 * slot + ch, 32, stride=4), :]
+                high[rows, lanes], low[rows, lanes] = split(value)
+
+
+def gather_kernel(place, *refs):
+    parts, (high, low) = refs[:7], refs[7:]
+    last = (place[1] // 4 + 4) % 8 // 2
+    rows = pl.ds(pl.multiple_of(last * 512, 512), 512)
+    high[rows, :] = jnp.zeros((512, 512), jnp.bfloat16)
+    low[rows, :] = jnp.zeros((512, 512), jnp.bfloat16)
+    for g in range(7):
+        place_part(place, g, lambda u, g=g: (parts[g], 256 * u), high, low, 1)
+
+
+def gather(place, parts):
+    wide = jax.ShapeDtypeStruct((2048, 512), jnp.bfloat16)
+    return pl.pallas_call(
+        gather_kernel,
+        out_shape=(wide, wide),
+        in_specs=[SMEM] + [VMEM] * 7,
+        out_specs=(VMEM, VMEM),
+        compiler_params=pltpu.CompilerParams(vmem_limit_bytes=24 << 20),
+        cost_estimate=pl.CostEstimate(flops=8_000_000_000, bytes_accessed=8 << 20, transcendentals=0),
+        name="gather",
+    )(place, *parts)
+
+
+def update_kernel(place, a, high, low, end0, end1, mine, other, upper, inverse, *refs):
+    out, weight, more_high, more_low, w_both = refs
     r = pl.program_id(0)
     p, s = place[0], place[1]
 
     @pl.when(r == 0)
     def _():
-        for g in range(8):
-            zz = (s // 4 + 8 - FAR_Z[g]) % 8
-            q, late = zz // 2, jnp.where(zz % 2 == p // 4, 0, 32)
-            for u in range(4):
-                yy = (s % 4 + 4 - FAR_Y[u]) % 4
-                part, first = (parts[g], 256 * u) if g < 7 else (parts[7 + u // 2], 256 * (u % 2))
-                for slot in range(2):
-                    if slot == 0:
-                        k = jnp.where(yy < 2, 64 * yy, 128 + 64 * yy) + late
-                    else:
-                        k = jnp.where(yy < 2, 384 + 64 * yy, 64 * yy) + late
-                    rows = pl.ds(pl.multiple_of(q * 512 + k, 32), 32)
-                    for ch in range(4):
-                        lanes = slice(128 * ch, 128 * ch + 128)
-                        value = part[pl.ds(first + 128 * slot + ch, 32, stride=4), :]
-                        high[rows, lanes], low[rows, lanes] = split(value)
+        more_high[...] = jnp.zeros((512, 512), jnp.bfloat16)
+        more_low[...] = jnp.zeros((512, 512), jnp.bfloat16)
+        ends = (end0, end1)
+        place_part(place, 7, lambda u: (ends[u // 2], 256 * (u % 2)), more_high, more_low, 0)
         odd = p % 2 == 1
         for ch in range(4):
             lanes = slice(128 * ch, 128 * ch + 128)
@@ -287,16 +317,21 @@
         col = lax.broadcasted_iota(jnp.int32, (512, 512), 1)
         pick = jnp.where(row == col + 256 * s, -1.0, 0.0)
         half = jnp.where((col < 256) & (s < 2), pick, half)
-        w_high[...], w_low[...] = split(dot(inverse[...], half, ((0,), (0,))))
+        w_both[:, 0:512], w_both[:, 512:1024] = split(dot(inverse[...], half, ((0,), (0,))))
 
     c, q = r // 4, r % 4
-    block = (pl.ds(pl.multiple_of(q * 512, 512), 512), pl.ds(pl.multiple_of(c * 256, 256), 256))
-    x_high, x_low = high[block], low[block]
+    lanes = pl.ds(pl.multiple_of(c * 256, 256), 256)
+    block = (pl.ds(pl.multiple_of(q * 512, 512), 512), lanes)
+    last = q == (s // 4 + 4) % 8 // 2
+    zero = jnp.zeros((512, 256), jnp.bfloat16)
+    x_high = high[block] + jnp.where(last, more_high[:, lanes], zero)
+    x_low = low[block] + jnp.where(last, more_low[:, lanes], zero)
 
     def times(x, w):
         return lax.dot_general(x, w, (((0,), (0,)), ((), ())), preferred_element_type=jnp.float32)
 
-    product = times(x_high, w_high[...]) + (times(x_high, w_low[...]) + times(x_low, w_high[...]))
+    both = times(x_high, w_both[...])
+    product = both[:, 0:512] + (both[:, 512:1024] + times(x_low, w_both[:, 0:512]))
     for ch in range(4):
         kept = a[pl.ds(ch, 256, stride=4), :]
         if ch < 2:
@@ -315,24 +350,23 @@
                 out[where, :] = jnp.where(s == p, diagonal, jnp.where(s > p, 0.0, natural))
 
 
-def update(place, a, parts, mine, other, upper, inverse):
+def update(place, a, high, low, ends, mine, other, upper, inverse):
     return pl.pallas_call(
         update_kernel,
         out_shape=jax.ShapeDtypeStruct(a.shape, jnp.float32),
         grid=(8,),
-        in_specs=[SMEM, pl.BlockSpec((1024, 128), lambda r: (r, 0))] + [VMEM] * 13,
+        in_specs=[SMEM, pl.BlockSpec((1024, 128), lambda r: (r, 0))] + [VMEM] * 8,
         out_specs=pl.BlockSpec((1024, 128), lambda r: (r, 0)),
         scratch_shapes=[
             pltpu.VMEM((512, 512), jnp.float32),
-            pltpu.VMEM((2048, 512), jnp.bfloat16),
-            pltpu.VMEM((2048, 512), jnp.bfloat16),
             pltpu.VMEM((512, 512), jnp.bfloat16),
             pltpu.VMEM((512, 512), jnp.bfloat16),
+            pltpu.VMEM((512, 1024), jnp.bfloat16),
         ],
         compiler_params=pltpu.CompilerParams(vmem_limit_bytes=40 << 20),
         cost_estimate=pl.CostEstimate(flops=8_000_000_000, bytes_accessed=16 << 20, transcendentals=0),
         name="update",
-    )(place, a, *parts, mine, other, upper, inverse)
+    )(place, a, high, low, *ends, mine, other, upper, inverse)
 
 
 def per_device(kernel):
@@ -383,11 +417,11 @@
     up3, down3, upper, inverse = together(up3, down3, upper, inverse)
 
     up4, down4 = shifted(up3[:512], dz=1), shifted(down3[512:], dz=7)
-    up4, down4, *mine = together(up4, down4, *mine)
+    high, low = gather(place, [column, up1, down1, up2, down2, up3, down3])
+    up4, down4, high, low, *mine = together(up4, down4, high, low, *mine)
     mine = jnp.where(p < 2, own, sum(mine))
     other = swap_cores(mine)
-    parts = [column, up1, down1, up2, down2, up3, down3, up4, down4]
-    out = update(place, a, parts, mine, other, upper, inverse)
+    out = update(place, a, high, low, (up4, down4), mine, other, upper, inverse)
     return out.reshape(kernel.shape)
 
 

time: 134 us -> 132 us (0.985)
  waiting for transfers between devices: 29.1 us -> 24.1 us
  starting transfers between devices: 64.2 us -> 66.8 us
    ppermute x42, waiting for transfers between devices: 29.1 us -> 24.1 us  [send(): return lax.ppermute(value, AXES, flat)]
    ppermute x42, starting transfers between devices: 64.2 us -> 66.8 us  [send(): return lax.ppermute(value, AXES, flat)]
  transfers between devices with their start and end apart: 42 -> 42, of which waited for: 11 -> 6; matrix products, arithmetic and copies ran while one was open for 2% -> 2% of each run, Pallas kernels for 18% -> 19%
where the time goes in v3:
time: 132 us
  starting transfers between devices  66.8 us (51%)
  Pallas kernels  35.5 us (27%)
  waiting for transfers between devices  24.1 us (18%)
  local copies, waits for them, and re-layouts  3.8 us (3%)
    ppermute x42, starting transfers between devices, send(): return lax.ppermute(value, AXES, flat)  66.8 us
    ppermute x42, waiting for transfers between devices, send(): return lax.ppermute(value, AXES, flat)  24.1 us
    pallas_call x1, Pallas kernels, factor_second(): pl.pallas_call(factor_second_kernel, out_shape=(jax.ShapeDtypeStruct((2,...  12.9 us
    pallas_call x1, Pallas kernels, update(): pl.pallas_call(update_kernel, out_shape=jax.ShapeDtypeStruct(a.shape, jnp...  10.9 us
    pallas_call x1, Pallas kernels, factor_first(): pl.pallas_call(factor_first_kernel, out_shape=(block, block), in_specs=[V...  10.5 us
  transfers between devices with their start and end apart: 42, of which 6 were waited for; matrix products, arithmetic and copies ran while one was open for 2% of the time, Pallas kernels for 19%

profile of v3, /device:TPU:1, one launch (start us, length us, event | category | flops | bytes accessed | tf_op | source)
XLA Modules:
  0.0 131.7 jit_solution(638877184255522494)
XLA Ops:
  0.0 1.5 %fusion = (f32[1,1,64,2,1,256]{5,4,3,2,1,0:T(1,128)S(1)}, f32[1,1,64,2,1,256]{5,4,3,2,1,0:T(1,128)S(1)}, f32[1,1,64,2,1,256]{5,4,3,2,1,0:T(1,128)S(1)}, f32[1,1,64,2,1,256]{5,4,3,2,1,0:T(1,128)S(1)}) fusion(f32[8,1,256,2,1,256]{5,4,3,2,1,0:T(1,128)} %param.1), kind=kLoop, calls=%fused_computation.14 | loop fusion | bytes 1048576 | tf_op jit(solution)/shard_map/slice | solution.py:75
  1.5 6.2 %collective-permute-start = (f32[256,128]{1,0:T(8,128)S(1)}, f32[256,128]{1,0:T(8,128)S(1)}, u32[]{:S(2)}, u32[]{:S(2)}) collective-permute-start(f32[256,128]{1,0:T(8,128)S(1)} %bitcast.32), channel_id=1, source_target_pairs={{0,0},{32,2},{1,32},{33,34},{2,64},{34,66},{3,96},{35,98},{4,132},... | collective-permute-start | bytes 393224 | tf_op jit(solution)/shard_map/ppermute | solution.py:21
  7.7 2.3 %collective-permute-start.1 = (f32[256,128]{1,0:T(8,128)S(1)}, f32[256,128]{1,0:T(8,128)S(1)}, u32[]{:S(2)}, u32[]{:S(2)}) collective-permute-start(f32[256,128]{1,0:T(8,128)S(1)} %bitcast.31), channel_id=1, source_target_pairs={{0,1},{32,3},{1,33},{33,35},{2,65},{34,67},{3,97},{35,99},{4,133},... | collective-permute-start | bytes 393224 | tf_op jit(solution)/shard_map/ppermute | solution.py:21
  10.0 1.9 %collective-permute-start.2 = (f32[256,128]{1,0:T(8,128)S(1)}, f32[256,128]{1,0:T(8,128)S(1)}, u32[]{:S(2)}, u32[]{:S(2)}) collective-permute-start(f32[256,128]{1,0:T(8,128)S(1)} %bitcast.30), channel_id=1, source_target_pairs={{0,2},{32,0},{1,34},{33,32},{2,66},{34,64},{3,98},{35,96},{4,134},... | collective-permute-start | bytes 393224 | tf_op jit(solution)/shard_map/ppermute | solution.py:21
  11.9 2.1 %collective-permute-start.3 = (f32[256,128]{1,0:T(8,128)S(1)}, f32[256,128]{1,0:T(8,128)S(1)}, u32[]{:S(2)}, u32[]{:S(2)}) collective-permute-start(f32[256,128]{1,0:T(8,128)S(1)} %bitcast.29), channel_id=1, source_target_pairs={{0,3},{32,1},{1,35},{33,33},{2,67},{34,65},{3,99},{35,97},{4,135},... | collective-permute-start | bytes 393224 | tf_op jit(solution)/shard_map/ppermute | solution.py:21
  14.1 1.4 %slice.75 = f32[1,1,256,2,1,256]{5,4,3,2,1,0:T(1,128)S(1)} slice(f32[8,1,256,2,1,256]{5,4,3,2,1,0:T(1,128)} %param.1), slice={[0:1], [0:1], [0:256], [0:2], [0:1], [0:256]} | slice | bytes 1048576 | tf_op jit(solution)/shard_map/slice | solution.py:376
  22.9 4.4 %collective-permute-start.4 = (f32[256,128]{1,0:T(8,128)S(1)}, f32[256,128]{1,0:T(8,128)S(1)}, u32[]{:S(2)}, u32[]{:S(2)}) collective-permute-start(f32[256,128]{1,0:T(8,128)S(1)} %pad_maximum_fusion.2), channel_id=1, source_target_pairs={{0,4},{1,5},{2,6},{3,7},{8,12},{9,13},{10,14},{11,15},{16,20},{17,... | collective-permute-start | bytes 393224 | tf_op jit(solution)/shard_map/ppermute | solution.py:21
  28.7 4.0 %collective-permute-start.18 = (f32[512,128]{1,0:T(8,128)S(1)}, f32[512,128]{1,0:T(8,128)S(1)}, u32[]{:S(2)}, u32[]{:S(2)}) collective-permute-start(f32[512,128]{1,0:T(8,128)S(1)} %add_select_fusion.1), channel_id=1, source_target_pairs={{0,12},{1,13},{2,14},{3,15},{32,44},{33,45},{34,46},{35,47}} | collective-permute-start | bytes 786440 | tf_op jit(solution)/shard_map/ppermute | solution.py:21
  32.8 2.8 %collective-permute-start.19 = (f32[512,128]{1,0:T(8,128)S(1)}, f32[512,128]{1,0:T(8,128)S(1)}, u32[]{:S(2)}, u32[]{:S(2)}) collective-permute-start(f32[512,128]{1,0:T(8,128)S(1)} %add_select_fusion.1), channel_id=1, source_target_pairs={{0,20},{1,21},{2,22},{3,23},{32,52},{33,53},{34,54},{35,55}} | collective-permute-start | bytes 786440 | tf_op jit(solution)/shard_map/ppermute | solution.py:21
  36.1 2.3 %collective-permute-start.13 = (f32[256,128]{1,0:T(8,128)S(1)}, f32[256,128]{1,0:T(8,128)S(1)}, u32[]{:S(2)}, u32[]{:S(2)}) collective-permute-start(f32[256,128]{1,0:T(8,128)S(1)} %maximum_select_fusion), channel_id=1, source_target_pairs={{0,3},{1,0},{2,1},{3,2},{4,7},{5,4},{6,5},{7,6},{8,11},{9,8},{10,9... | collective-permute-start | bytes 393224 | tf_op jit(solution)/shard_map/ppermute | solution.py:21
  39.4 1.5 %collective-permute-done.19 = f32[512,128]{1,0:T(8,128)S(1)} collective-permute-done((f32[512,128]{1,0:T(8,128)S(1)}, f32[512,128]{1,0:T(8,128)S(1)}, u32[]{:S(2)}, u32[]{:S(2)}) %collective-permute-start.19) | collective-permute-done | bytes 262176 | tf_op jit(solution)/shard_map/ppermute | solution.py:21
  42.4 1.9 %collective-permute-done.13 = f32[256,128]{1,0:T(8,128)S(1)} collective-permute-done((f32[256,128]{1,0:T(8,128)S(1)}, f32[256,128]{1,0:T(8,128)S(1)}, u32[]{:S(2)}, u32[]{:S(2)}) %collective-permute-start.13) | collective-permute-done | bytes 131104 | tf_op jit(solution)/shard_map/ppermute | solution.py:21
  44.4 2.7 %collective-permute-start.21 = (f32[1024,128]{1,0:T(8,128)S(1)}, f32[1024,128]{1,0:T(8,128)S(1)}, u32[]{:S(2)}, u32[]{:S(2)}) collective-permute-start(f32[1024,128]{1,0:T(8,128)S(1)} %pad_maximum_fusion.refs_0_), channel_id=1, source_target_pairs={{0,28},{1,29},{2,30},{3,31},{4,0},{5,1},{6,2},{7,3},{8,4},{9,5},{1... | collective-permute-start | bytes 1572872 | tf_op jit(solution)/shard_map/ppermute | solution.py:21
  47.1 1.3 collective-permute-start.26
  48.4 1.3 collective-permute-start.27
  51.1 14.5 %collective-permute-done.25.other = f32[384,128]{1,0:T(8,128)S(1)} collective-permute-done((f32[384,128]{1,0:T(8,128)S(1)}, f32[384,128]{1,0:T(8,128)S(1)}, u32[]{:S(2)}, u32[]{:S(2)}) %collective-permute-start.25) | collective-permute-done | bytes 196640 | tf_op jit(solution)/shard_map/ppermute | solution.py:21
  65.7 1.3 collective-permute-start.30
  67.0 1.3 collective-permute-start.31
  68.3 1.3 collective-permute-start.32
  69.7 2.7 %collective-permute-start.29 = (f32[1024,128]{1,0:T(8,128)S(1)}, f32[1024,128]{1,0:T(8,128)S(1)}, u32[]{:S(2)}, u32[]{:S(2)}) collective-permute-start(f32[1024,128]{1,0:T(8,128)S(1)} %collective-permute-done.21.refs_2_), channel_id=1, source_target_pairs={{0,28},{1,29},{2,30},{3,31},{4,0},{5,1},{6,2},{7,3},{8,4},{9,5},{1... | collective-permute-start | bytes 1572872 | tf_op jit(solution)/shard_map/ppermute | solution.py:21
  72.4 10.5 %factor_first.1 = (f32[256,256]{1,0:T(8,128)S(1)}, f32[256,256]{1,0:T(8,128)S(1)}) custom-call(f32[384,128]{1,0:T(8,128)S(1)} %add_add_fusion.3.mine, f32[384,128]{1,0:T(8,128)S(1)} %collective-permute-done.25.other), custom_call_target="tpu_custom_call" | custom-call | flops 60000002048 | bytes 1048576 | tf_op jit(solution)/shard_map/factor_first/pallas_call | solution.py:219
  83.0 6.0 %collective-permute-start.35 = (f32[512,128]{1,0:T(8,128)S(1)}, f32[512,128]{1,0:T(8,128)S(1)}, u32[]{:S(2)}, u32[]{:S(2)}) collective-permute-start(f32[512,128]{1,0:T(8,128)S(1)} %add_add_fusion.mine), channel_id=1, source_target_pairs={{0,32},{1,33},{2,34},{3,35},{4,36},{5,37},{6,38},{7,39},{8,40},{9,... | collective-permute-start | bytes 786440 | tf_op jit(solution)/shard_map/ppermute | solution.py:21
  89.0 1.3 collective-permute-start.38
  90.3 1.3 %collective-permute-start.39 = (f32[1024,128]{1,0:T(8,128)S(1)}, f32[1024,128]{1,0:T(8,128)S(1)}, u32[]{:S(2)}, u32[]{:S(2)}) collective-permute-start(f32[1024,128]{1,0:T(8,128)S(1)} %bitcast.15), channel_id=1, source_target_pairs={{0,192},{1,193},{2,194},{3,195},{4,196},{5,197},{6,198},{7,199},{8... | collective-permute-start | bytes 1572872 | tf_op jit(solution)/shard_map/ppermute | solution.py:21
  91.7 1.3 %collective-permute-start.40 = (f32[1024,128]{1,0:T(8,128)S(1)}, f32[1024,128]{1,0:T(8,128)S(1)}, u32[]{:S(2)}, u32[]{:S(2)}) collective-permute-start(f32[1024,128]{1,0:T(8,128)S(1)} %bitcast.16), channel_id=1, source_target_pairs={{0,128},{1,129},{2,130},{3,131},{4,132},{5,133},{6,134},{7,135},{8... | collective-permute-start | bytes 1572872 | tf_op jit(solution)/shard_map/ppermute | solution.py:21
  93.1 2.7 %collective-permute-start.34 = (f32[1024,128]{1,0:T(8,128)S(1)}, f32[1024,128]{1,0:T(8,128)S(1)}, u32[]{:S(2)}, u32[]{:S(2)}) collective-permute-start(f32[1024,128]{1,0:T(8,128)S(1)} %collective-permute-done.29.refs_4_), channel_id=1, source_target_pairs={{0,28},{1,29},{2,30},{3,31},{4,0},{5,1},{6,2},{7,3},{8,4},{9,5},{1... | collective-permute-start | bytes 1572872 | tf_op jit(solution)/shard_map/ppermute | solution.py:21
  95.8 12.9 %factor_second.1 = (f32[2,256,256]{2,1,0:T(8,128)S(1)}, f32[512,512]{1,0:T(8,128)S(1)}) custom-call(s32[2]{0:T(128)S(1)} %pad_add_fusion.place, f32[512,128]{1,0:T(8,128)S(1)} %add_add_fusion.mine, f32[512,128]{1,0:T(8,128)S(1)} %collective-permute-done.35.other, f32[256,256]{1,0:T(8,128)S(1)} %get-tuple-element.63.upper0, ...), custom_call_target="tpu_custom_call" | custom-call | flops 60000002048 | bytes 1048576 | tf_op jit(solution)/shard_map/factor_second/pallas_call | solution.py:232
  108.8 2.7 %collective-permute-start.37 = (f32[512,128]{1,0:T(8,128)S(1)}, f32[512,128]{1,0:T(8,128)S(1)}, u32[]{:S(2)}, u32[]{:S(2)}) collective-permute-start(f32[512,128]{1,0:T(8,128)S(1)} %slice.80), channel_id=1, source_target_pairs={{0,28},{1,29},{2,30},{3,31},{4,0},{5,1},{6,2},{7,3},{8,4},{9,5},{1... | collective-permute-start | bytes 786440 | tf_op jit(solution)/shard_map/ppermute | solution.py:21
  113.1 4.2 %collective-permute-done.36.end0 = f32[512,128]{1,0:T(8,128)S(1)} collective-permute-done((f32[512,128]{1,0:T(8,128)S(1)}, f32[512,128]{1,0:T(8,128)S(1)}, u32[]{:S(2)}, u32[]{:S(2)}) %collective-permute-start.36) | collective-permute-done | bytes 262176 | tf_op jit(solution)/shard_map/ppermute | solution.py:21
  117.4 1.8 %collective-permute-start.41 = (f32[1024,128]{1,0:T(8,128)S(1)}, f32[1024,128]{1,0:T(8,128)S(1)}, u32[]{:S(2)}, u32[]{:S(2)}) collective-permute-start(f32[1024,128]{1,0:T(8,128)S(1)} %add_select_fusion.mine), channel_id=1, source_target_pairs={{0,32},{1,33},{2,34},{3,35},{4,36},{5,37},{6,38},{7,39},{8,40},{9,... | collective-permute-start | bytes 1572872 | tf_op jit(solution)/shard_map/ppermute | solution.py:21
  119.2 1.5 %collective-permute-done.41.other = f32[1024,128]{1,0:T(8,128)S(1)} collective-permute-done((f32[1024,128]{1,0:T(8,128)S(1)}, f32[1024,128]{1,0:T(8,128)S(1)}, u32[]{:S(2)}, u32[]{:S(2)}) %collective-permute-start.41) | collective-permute-done | bytes 524320 | tf_op jit(solution)/shard_map/ppermute | solution.py:21
  120.7 10.9 %update.1 = f32[8192,128]{1,0:T(8,128)} custom-call(s32[2]{0:T(128)S(1)} %pad_add_fusion.place, f32[8192,128]{1,0:T(8,128)S(1)} %bitcast.13, bf16[2048,512]{1,0:T(8,128)(2,1)S(1)} %get-tuple-element.72.high, bf16[2048,512]{1,0:T(8,128)(2,1)S(1)} %get-tuple-element.73.low, f32[512,128]{1,0:T(8,128)S(1)} %collective-permute-done.36.end0, ...), custom_call_target="tpu_custom_call" | custom-call | flops 8000000000 | bytes 16777216 | tf_op jit(solution)/shard_map/update/pallas_call | solution.py:354
  (87 shorter events, 14.9 us)
Async XLA Ops:
  1.5 15.8 %collective-permute-start = (f32[256,128]{1,0:T(8,128)S(1)}, f32[256,128]{1,0:T(8,128)S(1)}, u32[]{:S(2)}, u32[]{:S(2)}) collective-permute-start(f32[256,128]{1,0:T(8,128)S(1)} %bitcast.32), channel_id=1, source_target_pairs={{0,0},{32,2},{1,32},{33,34},{2,64},{34,66},{3,96},{35,98},{4,132},... | collective-permute-start | bytes 393224 | tf_op jit(solution)/shard_map/ppermute | solution.py:21
  7.7 10.2 %collective-permute-start.1 = (f32[256,128]{1,0:T(8,128)S(1)}, f32[256,128]{1,0:T(8,128)S(1)}, u32[]{:S(2)}, u32[]{:S(2)}) collective-permute-start(f32[256,128]{1,0:T(8,128)S(1)} %bitcast.31), channel_id=1, source_target_pairs={{0,1},{32,3},{1,33},{33,35},{2,65},{34,67},{3,97},{35,99},{4,133},... | collective-permute-start | bytes 393224 | tf_op jit(solution)/shard_map/ppermute | solution.py:21
  10.0 8.6 %collective-permute-start.2 = (f32[256,128]{1,0:T(8,128)S(1)}, f32[256,128]{1,0:T(8,128)S(1)}, u32[]{:S(2)}, u32[]{:S(2)}) collective-permute-start(f32[256,128]{1,0:T(8,128)S(1)} %bitcast.30), channel_id=1, source_target_pairs={{0,2},{32,0},{1,34},{33,32},{2,66},{34,64},{3,98},{35,96},{4,134},... | collective-permute-start | bytes 393224 | tf_op jit(solution)/shard_map/ppermute | solution.py:21
  19.5 7.8 %collective-permute-start.9 = (f32[384,128]{1,0:T(8,128)S(1)}, f32[384,128]{1,0:T(8,128)S(1)}, u32[]{:S(2)}, u32[]{:S(2)}) collective-permute-start(f32[384,128]{1,0:T(8,128)S(1)} %add_select_fusion.2), channel_id=1, source_target_pairs={{0,20},{1,21},{2,22},{3,23}} | collective-permute-start | bytes 589832 | tf_op jit(solution)/shard_map/ppermute | solution.py:21
  20.2 7.8 %collective-permute-start.15 = (f32[512,128]{1,0:T(8,128)S(1)}, f32[512,128]{1,0:T(8,128)S(1)}, u32[]{:S(2)}, u32[]{:S(2)}) collective-permute-start(f32[512,128]{1,0:T(8,128)S(1)} %bitcast.23), channel_id=1, source_target_pairs={{1,2},{33,34}} | collective-permute-start | bytes 786440 | tf_op jit(solution)/shard_map/ppermute | solution.py:21
  20.8 7.8 %collective-permute-start.16 = (f32[512,128]{1,0:T(8,128)S(1)}, f32[512,128]{1,0:T(8,128)S(1)}, u32[]{:S(2)}, u32[]{:S(2)}) collective-permute-start(f32[512,128]{1,0:T(8,128)S(1)} %bitcast.24), channel_id=1, source_target_pairs={{1,0},{33,32}} | collective-permute-start | bytes 786440 | tf_op jit(solution)/shard_map/ppermute | solution.py:21
  22.9 12.7 %collective-permute-start.4 = (f32[256,128]{1,0:T(8,128)S(1)}, f32[256,128]{1,0:T(8,128)S(1)}, u32[]{:S(2)}, u32[]{:S(2)}) collective-permute-start(f32[256,128]{1,0:T(8,128)S(1)} %pad_maximum_fusion.2), channel_id=1, source_target_pairs={{0,4},{1,5},{2,6},{3,7},{8,12},{9,13},{10,14},{11,15},{16,20},{17,... | collective-permute-start | bytes 393224 | tf_op jit(solution)/shard_map/ppermute | solution.py:21
  27.3 8.3 %collective-permute-start.10 = (f32[384,128]{1,0:T(8,128)S(1)}, f32[384,128]{1,0:T(8,128)S(1)}, u32[]{:S(2)}, u32[]{:S(2)}) collective-permute-start(f32[384,128]{1,0:T(8,128)S(1)} %add_add_fusion.5), channel_id=1, source_target_pairs={{0,4},{1,5},{2,6},{3,7},{12,16},{13,17},{14,18},{15,19},{20,24},{2... | collective-permute-start | bytes 589832 | tf_op jit(solution)/shard_map/ppermute | solution.py:21
  28.0 7.6 %collective-permute-start.11 = (f32[384,128]{1,0:T(8,128)S(1)}, f32[384,128]{1,0:T(8,128)S(1)}, u32[]{:S(2)}, u32[]{:S(2)}) collective-permute-start(f32[384,128]{1,0:T(8,128)S(1)} %add_add_fusion.5), channel_id=1, source_target_pairs={{0,28},{1,29},{2,30},{3,31},{12,8},{13,9},{14,10},{15,11}} | collective-permute-start | bytes 589832 | tf_op jit(solution)/shard_map/ppermute | solution.py:21
  28.7 10.0 %collective-permute-start.18 = (f32[512,128]{1,0:T(8,128)S(1)}, f32[512,128]{1,0:T(8,128)S(1)}, u32[]{:S(2)}, u32[]{:S(2)}) collective-permute-start(f32[512,128]{1,0:T(8,128)S(1)} %add_select_fusion.1), channel_id=1, source_target_pairs={{0,12},{1,13},{2,14},{3,15},{32,44},{33,45},{34,46},{35,47}} | collective-permute-start | bytes 786440 | tf_op jit(solution)/shard_map/ppermute | solution.py:21
  32.8 8.2 %collective-permute-start.19 = (f32[512,128]{1,0:T(8,128)S(1)}, f32[512,128]{1,0:T(8,128)S(1)}, u32[]{:S(2)}, u32[]{:S(2)}) collective-permute-start(f32[512,128]{1,0:T(8,128)S(1)} %add_select_fusion.1), channel_id=1, source_target_pairs={{0,20},{1,21},{2,22},{3,23},{32,52},{33,53},{34,54},{35,55}} | collective-permute-start | bytes 786440 | tf_op jit(solution)/shard_map/ppermute | solution.py:21
  36.1 8.2 %collective-permute-start.13 = (f32[256,128]{1,0:T(8,128)S(1)}, f32[256,128]{1,0:T(8,128)S(1)}, u32[]{:S(2)}, u32[]{:S(2)}) collective-permute-start(f32[256,128]{1,0:T(8,128)S(1)} %maximum_select_fusion), channel_id=1, source_target_pairs={{0,3},{1,0},{2,1},{3,2},{4,7},{5,4},{6,5},{7,6},{8,11},{9,8},{10,9... | collective-permute-start | bytes 393224 | tf_op jit(solution)/shard_map/ppermute | solution.py:21
  38.7 8.4 %collective-permute-start.22 = (f32[384,128]{1,0:T(8,128)S(1)}, f32[384,128]{1,0:T(8,128)S(1)}, u32[]{:S(2)}, u32[]{:S(2)}) collective-permute-start(f32[384,128]{1,0:T(8,128)S(1)} %add_add_fusion.4), channel_id=1, source_target_pairs={{0,64},{1,65},{2,66},{3,67},{4,68},{5,69},{6,70},{7,71},{8,72},{9,... | collective-permute-start | bytes 589832 | tf_op jit(solution)/shard_map/ppermute | solution.py:21
  41.7 8.1 %collective-permute-start.24 = (f32[384,128]{1,0:T(8,128)S(1)}, f32[384,128]{1,0:T(8,128)S(1)}, u32[]{:S(2)}, u32[]{:S(2)}) collective-permute-start(f32[384,128]{1,0:T(8,128)S(1)} %add_add_fusion.4), channel_id=1, source_target_pairs={{0,128},{1,129},{2,130},{3,131},{4,132},{5,133},{6,134},{7,135},{8... | collective-permute-start | bytes 589832 | tf_op jit(solution)/shard_map/ppermute | solution.py:21
  44.4 21.3 %collective-permute-start.20 = (f32[1024,128]{1,0:T(8,128)S(1)}, f32[1024,128]{1,0:T(8,128)S(1)}, u32[]{:S(2)}, u32[]{:S(2)}) collective-permute-start(f32[1024,128]{1,0:T(8,128)S(1)} %pad_maximum_fusion.refs_0_), channel_id=1, source_target_pairs={{0,4},{1,5},{2,6},{3,7},{4,8},{5,9},{6,10},{7,11},{8,12},{9,13},{1... | collective-permute-start | bytes 1572872 | tf_op jit(solution)/shard_map/ppermute | solution.py:21
  44.4 21.2 %collective-permute-start.21 = (f32[1024,128]{1,0:T(8,128)S(1)}, f32[1024,128]{1,0:T(8,128)S(1)}, u32[]{:S(2)}, u32[]{:S(2)}) collective-permute-start(f32[1024,128]{1,0:T(8,128)S(1)} %pad_maximum_fusion.refs_0_), channel_id=1, source_target_pairs={{0,28},{1,29},{2,30},{3,31},{4,0},{5,1},{6,2},{7,3},{8,4},{9,5},{1... | collective-permute-start | bytes 1572872 | tf_op jit(solution)/shard_map/ppermute | solution.py:21
  47.1 18.5 %collective-permute-start.26 = (f32[512,128]{1,0:T(8,128)S(1)}, f32[512,128]{1,0:T(8,128)S(1)}, u32[]{:S(2)}, u32[]{:S(2)}) collective-permute-start(f32[512,128]{1,0:T(8,128)S(1)} %add_add_fusion.2), channel_id=1, source_target_pairs={{0,4},{1,5},{2,6},{3,7},{12,16},{13,17},{14,18},{15,19},{20,24},{2... | collective-permute-start | bytes 786440 | tf_op jit(solution)/shard_map/ppermute | solution.py:21
  48.4 17.2 %collective-permute-start.27 = (f32[512,128]{1,0:T(8,128)S(1)}, f32[512,128]{1,0:T(8,128)S(1)}, u32[]{:S(2)}, u32[]{:S(2)}) collective-permute-start(f32[512,128]{1,0:T(8,128)S(1)} %add_add_fusion.2), channel_id=1, source_target_pairs={{0,28},{1,29},{2,30},{3,31},{12,8},{13,9},{14,10},{15,11},{32,60},... | collective-permute-start | bytes 786440 | tf_op jit(solution)/shard_map/ppermute | solution.py:21
  49.8 15.8 %collective-permute-start.25 = (f32[384,128]{1,0:T(8,128)S(1)}, f32[384,128]{1,0:T(8,128)S(1)}, u32[]{:S(2)}, u32[]{:S(2)}) collective-permute-start(f32[384,128]{1,0:T(8,128)S(1)} %add_add_fusion.3.mine), channel_id=1, source_target_pairs={{0,32},{1,33},{2,34},{3,35},{4,36},{5,37},{6,38},{7,39},{8,40},{9,... | collective-permute-start | bytes 589832 | tf_op jit(solution)/shard_map/ppermute | solution.py:21
  65.7 17.2 %collective-permute-start.30 = (f32[512,128]{1,0:T(8,128)S(1)}, f32[512,128]{1,0:T(8,128)S(1)}, u32[]{:S(2)}, u32[]{:S(2)}) collective-permute-start(f32[512,128]{1,0:T(8,128)S(1)} %add_add_fusion.1), channel_id=1, source_target_pairs={{0,64},{1,65},{2,66},{3,67},{4,68},{5,69},{6,70},{7,71},{8,72},{9,... | collective-permute-start | bytes 786440 | tf_op jit(solution)/shard_map/ppermute | solution.py:21
  67.0 15.9 %collective-permute-start.31 = (f32[512,128]{1,0:T(8,128)S(1)}, f32[512,128]{1,0:T(8,128)S(1)}, u32[]{:S(2)}, u32[]{:S(2)}) collective-permute-start(f32[512,128]{1,0:T(8,128)S(1)} %add_add_fusion.1), channel_id=1, source_target_pairs={{0,192},{1,193},{2,194},{3,195},{4,196},{5,197},{6,198},{7,199},{8... | collective-permute-start | bytes 786440 | tf_op jit(solution)/shard_map/ppermute | solution.py:21
  68.3 14.6 %collective-permute-start.32 = (f32[512,128]{1,0:T(8,128)S(1)}, f32[512,128]{1,0:T(8,128)S(1)}, u32[]{:S(2)}, u32[]{:S(2)}) collective-permute-start(f32[512,128]{1,0:T(8,128)S(1)} %add_add_fusion.1), channel_id=1, source_target_pairs={{0,128},{1,129},{2,130},{3,131},{4,132},{5,133},{6,134},{7,135},{8... | collective-permute-start | bytes 786440 | tf_op jit(solution)/shard_map/ppermute | solution.py:21
  69.6 13.3 %collective-permute-start.28 = (f32[1024,128]{1,0:T(8,128)S(1)}, f32[1024,128]{1,0:T(8,128)S(1)}, u32[]{:S(2)}, u32[]{:S(2)}) collective-permute-start(f32[1024,128]{1,0:T(8,128)S(1)} %collective-permute-done.20.refs_1_), channel_id=1, source_target_pairs={{0,4},{1,5},{2,6},{3,7},{4,8},{5,9},{6,10},{7,11},{8,12},{9,13},{1... | collective-permute-start | bytes 1572872 | tf_op jit(solution)/shard_map/ppermute | solution.py:21
  69.7 13.2 %collective-permute-start.29 = (f32[1024,128]{1,0:T(8,128)S(1)}, f32[1024,128]{1,0:T(8,128)S(1)}, u32[]{:S(2)}, u32[]{:S(2)}) collective-permute-start(f32[1024,128]{1,0:T(8,128)S(1)} %collective-permute-done.21.refs_2_), channel_id=1, source_target_pairs={{0,28},{1,29},{2,30},{3,31},{4,0},{5,1},{6,2},{7,3},{8,4},{9,5},{1... | collective-permute-start | bytes 1572872 | tf_op jit(solution)/shard_map/ppermute | solution.py:21
  83.0 10.1 %collective-permute-start.35 = (f32[512,128]{1,0:T(8,128)S(1)}, f32[512,128]{1,0:T(8,128)S(1)}, u32[]{:S(2)}, u32[]{:S(2)}) collective-permute-start(f32[512,128]{1,0:T(8,128)S(1)} %add_add_fusion.mine), channel_id=1, source_target_pairs={{0,32},{1,33},{2,34},{3,35},{4,36},{5,37},{6,38},{7,39},{8,40},{9,... | collective-permute-start | bytes 786440 | tf_op jit(solution)/shard_map/ppermute | solution.py:21
  89.0 23.8 %collective-permute-start.38 = (f32[1024,128]{1,0:T(8,128)S(1)}, f32[1024,128]{1,0:T(8,128)S(1)}, u32[]{:S(2)}, u32[]{:S(2)}) collective-permute-start(f32[1024,128]{1,0:T(8,128)S(1)} %bitcast.14), channel_id=1, source_target_pairs={{0,64},{1,65},{2,66},{3,67},{4,68},{5,69},{6,70},{7,71},{8,72},{9,... | collective-permute-start | bytes 1572872 | tf_op jit(solution)/shard_map/ppermute | solution.py:21
  90.3 22.5 %collective-permute-start.39 = (f32[1024,128]{1,0:T(8,128)S(1)}, f32[1024,128]{1,0:T(8,128)S(1)}, u32[]{:S(2)}, u32[]{:S(2)}) collective-permute-start(f32[1024,128]{1,0:T(8,128)S(1)} %bitcast.15), channel_id=1, source_target_pairs={{0,192},{1,193},{2,194},{3,195},{4,196},{5,197},{6,198},{7,199},{8... | collective-permute-start | bytes 1572872 | tf_op jit(solution)/shard_map/ppermute | solution.py:21
  91.7 21.4 %collective-permute-start.40 = (f32[1024,128]{1,0:T(8,128)S(1)}, f32[1024,128]{1,0:T(8,128)S(1)}, u32[]{:S(2)}, u32[]{:S(2)}) collective-permute-start(f32[1024,128]{1,0:T(8,128)S(1)} %bitcast.16), channel_id=1, source_target_pairs={{0,128},{1,129},{2,130},{3,131},{4,132},{5,133},{6,134},{7,135},{8... | collective-permute-start | bytes 1572872 | tf_op jit(solution)/shard_map/ppermute | solution.py:21
  93.0 15.7 %collective-permute-start.33 = (f32[1024,128]{1,0:T(8,128)S(1)}, f32[1024,128]{1,0:T(8,128)S(1)}, u32[]{:S(2)}, u32[]{:S(2)}) collective-permute-start(f32[1024,128]{1,0:T(8,128)S(1)} %collective-permute-done.28.refs_3_), channel_id=1, source_target_pairs={{0,4},{1,5},{2,6},{3,7},{4,8},{5,9},{6,10},{7,11},{8,12},{9,13},{1... | collective-permute-start | bytes 1572872 | tf_op jit(solution)/shard_map/ppermute | solution.py:21
  93.1 15.6 %collective-permute-start.34 = (f32[1024,128]{1,0:T(8,128)S(1)}, f32[1024,128]{1,0:T(8,128)S(1)}, u32[]{:S(2)}, u32[]{:S(2)}) collective-permute-start(f32[1024,128]{1,0:T(8,128)S(1)} %collective-permute-done.29.refs_4_), channel_id=1, source_target_pairs={{0,28},{1,29},{2,30},{3,31},{4,0},{5,1},{6,2},{7,3},{8,4},{9,5},{1... | collective-permute-start | bytes 1572872 | tf_op jit(solution)/shard_map/ppermute | solution.py:21
  108.7 8.6 %collective-permute-start.36 = (f32[512,128]{1,0:T(8,128)S(1)}, f32[512,128]{1,0:T(8,128)S(1)}, u32[]{:S(2)}, u32[]{:S(2)}) collective-permute-start(f32[512,128]{1,0:T(8,128)S(1)} %slice.79), channel_id=1, source_target_pairs={{0,4},{1,5},{2,6},{3,7},{4,8},{5,9},{6,10},{7,11},{8,12},{9,13},{1... | collective-permute-start | bytes 786440 | tf_op jit(solution)/shard_map/ppermute | solution.py:21
  108.8 8.4 %collective-permute-start.37 = (f32[512,128]{1,0:T(8,128)S(1)}, f32[512,128]{1,0:T(8,128)S(1)}, u32[]{:S(2)}, u32[]{:S(2)}) collective-permute-start(f32[512,128]{1,0:T(8,128)S(1)} %slice.80), channel_id=1, source_target_pairs={{0,28},{1,29},{2,30},{3,31},{4,0},{5,1},{6,2},{7,3},{8,4},{9,5},{1... | collective-permute-start | bytes 786440 | tf_op jit(solution)/shard_map/ppermute | solution.py:21
  (11 other events, 56.6 us)

commit v4 on v3

--- a/solution.py
+++ b/solution.py
@@ -418,7 +418,7 @@
 
     up4, down4 = shifted(up3[:512], dz=1), shifted(down3[512:], dz=7)
     high, low = gather(place, [column, up1, down1, up2, down2, up3, down3])
-    up4, down4, high, low, *mine = together(up4, down4, high, low, *mine)
+    up4, down4, high, low = together(up4, down4, high, low)
     mine = jnp.where(p < 2, own, sum(mine))
     other = swap_cores(mine)
     out = update(place, a, high, low, (up4, down4), mine, other, upper, inverse)

time: 132 us -> 136 us (1.030)
  waiting for transfers between devices: 24.1 us -> 32.9 us
  starting transfers between devices: 66.8 us -> 61.3 us
    ppermute x42, waiting for transfers between devices: 24.1 us -> 32.9 us  [send(): return lax.ppermute(value, AXES, flat)]
    ppermute x42, starting transfers between devices: 66.8 us -> 61.3 us  [send(): return lax.ppermute(value, AXES, flat)]
  transfers between devices with their start and end apart: 42 -> 42, of which waited for: 6 -> 10; matrix products, arithmetic and copies ran while one was open for 2% -> 2% of each run, Pallas kernels for 19% -> 18%
where the time goes in v4:
time: 136 us; the launch traced here: 135 us
  starting transfers between devices  61.3 us (45%)
  Pallas kernels  35.6 us (26%)
  waiting for transfers between devices  32.9 us (24%)
  local copies, waits for them, and re-layouts  3.81 us (3%)
    ppermute x42, starting transfers between devices, send(): return lax.ppermute(value, AXES, flat)  61.3 us
    ppermute x42, waiting for transfers between devices, send(): return lax.ppermute(value, AXES, flat)  32.9 us
    pallas_call x1, Pallas kernels, factor_second(): pl.pallas_call(factor_second_kernel, out_shape=(jax.ShapeDtypeStruct((2,...  12.9 us
    pallas_call x1, Pallas kernels, update(): pl.pallas_call(update_kernel, out_shape=jax.ShapeDtypeStruct(a.shape, jnp...  11 us
    pallas_call x1, Pallas kernels, factor_first(): pl.pallas_call(factor_first_kernel, out_shape=(block, block), in_specs=[V...  10.5 us
  transfers between devices with their start and end apart: 42, of which 10 were waited for; matrix products, arithmetic and copies ran while one was open for 2% of the time, Pallas kernels for 18%

profile of v4, /device:TPU:1, one launch (start us, length us, event | category | flops | bytes accessed | tf_op | source)
XLA Modules:
  0.0 134.9 jit_solution(17896074274494869147)
XLA Ops:
  0.0 1.5 %fusion = (f32[1,1,64,2,1,256]{5,4,3,2,1,0:T(1,128)S(1)}, f32[1,1,64,2,1,256]{5,4,3,2,1,0:T(1,128)S(1)}, f32[1,1,64,2,1,256]{5,4,3,2,1,0:T(1,128)S(1)}, f32[1,1,64,2,1,256]{5,4,3,2,1,0:T(1,128)S(1)}) fusion(f32[8,1,256,2,1,256]{5,4,3,2,1,0:T(1,128)} %param.1), kind=kLoop, calls=%fused_computation.14 | loop fusion | bytes 1048576 | tf_op jit(solution)/shard_map/slice | solution.py:75
  1.5 6.0 %collective-permute-start.1 = (f32[256,128]{1,0:T(8,128)S(1)}, f32[256,128]{1,0:T(8,128)S(1)}, u32[]{:S(2)}, u32[]{:S(2)}) collective-permute-start(f32[256,128]{1,0:T(8,128)S(1)} %bitcast.32), channel_id=1, source_target_pairs={{0,1},{32,3},{1,33},{33,35},{2,65},{34,67},{3,97},{35,99},{4,133},... | collective-permute-start | bytes 393224 | tf_op jit(solution)/shard_map/ppermute | solution.py:21
  7.5 3.5 %collective-permute-start = (f32[256,128]{1,0:T(8,128)S(1)}, f32[256,128]{1,0:T(8,128)S(1)}, u32[]{:S(2)}, u32[]{:S(2)}) collective-permute-start(f32[256,128]{1,0:T(8,128)S(1)} %bitcast.31), channel_id=1, source_target_pairs={{0,0},{32,2},{1,32},{33,34},{2,64},{34,66},{3,96},{35,98},{4,132},... | collective-permute-start | bytes 393224 | tf_op jit(solution)/shard_map/ppermute | solution.py:21
  11.0 1.9 %collective-permute-start.2 = (f32[256,128]{1,0:T(8,128)S(1)}, f32[256,128]{1,0:T(8,128)S(1)}, u32[]{:S(2)}, u32[]{:S(2)}) collective-permute-start(f32[256,128]{1,0:T(8,128)S(1)} %bitcast.30), channel_id=1, source_target_pairs={{0,2},{32,0},{1,34},{33,32},{2,66},{34,64},{3,98},{35,96},{4,134},... | collective-permute-start | bytes 393224 | tf_op jit(solution)/shard_map/ppermute | solution.py:21
  12.9 2.4 %collective-permute-start.3 = (f32[256,128]{1,0:T(8,128)S(1)}, f32[256,128]{1,0:T(8,128)S(1)}, u32[]{:S(2)}, u32[]{:S(2)}) collective-permute-start(f32[256,128]{1,0:T(8,128)S(1)} %bitcast.29), channel_id=1, source_target_pairs={{0,3},{32,1},{1,35},{33,33},{2,67},{34,65},{3,99},{35,97},{4,135},... | collective-permute-start | bytes 393224 | tf_op jit(solution)/shard_map/ppermute | solution.py:21
  15.3 1.4 %slice.75 = f32[1,1,256,2,1,256]{5,4,3,2,1,0:T(1,128)S(1)} slice(f32[8,1,256,2,1,256]{5,4,3,2,1,0:T(1,128)} %param.1), slice={[0:1], [0:1], [0:256], [0:2], [0:1], [0:256]} | slice | bytes 1048576 | tf_op jit(solution)/shard_map/slice | solution.py:376
  24.1 4.0 %collective-permute-start.4 = (f32[256,128]{1,0:T(8,128)S(1)}, f32[256,128]{1,0:T(8,128)S(1)}, u32[]{:S(2)}, u32[]{:S(2)}) collective-permute-start(f32[256,128]{1,0:T(8,128)S(1)} %pad_maximum_fusion.2), channel_id=1, source_target_pairs={{0,4},{1,5},{2,6},{3,7},{8,12},{9,13},{10,14},{11,15},{16,20},{17,... | collective-permute-start | bytes 393224 | tf_op jit(solution)/shard_map/ppermute | solution.py:21
  29.5 1.6 %collective-permute-done.16 = f32[512,128]{1,0:T(8,128)S(1)} collective-permute-done((f32[512,128]{1,0:T(8,128)S(1)}, f32[512,128]{1,0:T(8,128)S(1)}, u32[]{:S(2)}, u32[]{:S(2)}) %collective-permute-start.16) | collective-permute-done | bytes 262176 | tf_op jit(solution)/shard_map/ppermute | solution.py:21
  31.2 4.6 %collective-permute-start.19 = (f32[512,128]{1,0:T(8,128)S(1)}, f32[512,128]{1,0:T(8,128)S(1)}, u32[]{:S(2)}, u32[]{:S(2)}) collective-permute-start(f32[512,128]{1,0:T(8,128)S(1)} %add_select_fusion.1), channel_id=1, source_target_pairs={{0,20},{1,21},{2,22},{3,23},{32,52},{33,53},{34,54},{35,55}} | collective-permute-start | bytes 786440 | tf_op jit(solution)/shard_map/ppermute | solution.py:21
  35.8 1.3 collective-permute-start.18
  38.5 1.4 %collective-permute-start.14 = (f32[256,128]{1,0:T(8,128)S(1)}, f32[256,128]{1,0:T(8,128)S(1)}, u32[]{:S(2)}, u32[]{:S(2)}) collective-permute-start(f32[256,128]{1,0:T(8,128)S(1)} %maximum_select_fusion), channel_id=1, source_target_pairs={{0,2},{1,3},{2,0},{3,1},{4,6},{5,7},{6,4},{7,5},{8,10},{9,11},{10,... | collective-permute-start | bytes 393224 | tf_op jit(solution)/shard_map/ppermute | solution.py:21
  41.2 1.3 collective-permute-done.18
  45.0 2.5 %collective-permute-done.12 = f32[256,128]{1,0:T(8,128)S(1)} collective-permute-done((f32[256,128]{1,0:T(8,128)S(1)}, f32[256,128]{1,0:T(8,128)S(1)}, u32[]{:S(2)}, u32[]{:S(2)}) %collective-permute-start.12) | collective-permute-done | bytes 131104 | tf_op jit(solution)/shard_map/ppermute | solution.py:21
  47.6 1.5 %collective-permute-start.20 = (f32[1024,128]{1,0:T(8,128)S(1)}, f32[1024,128]{1,0:T(8,128)S(1)}, u32[]{:S(2)}, u32[]{:S(2)}) collective-permute-start(f32[1024,128]{1,0:T(8,128)S(1)} %pad_maximum_fusion.refs_0_), channel_id=1, source_target_pairs={{0,4},{1,5},{2,6},{3,7},{4,8},{5,9},{6,10},{7,11},{8,12},{9,13},{1... | collective-permute-start | bytes 1572872 | tf_op jit(solution)/shard_map/ppermute | solution.py:21
  49.1 3.2 %collective-permute-start.27 = (f32[512,128]{1,0:T(8,128)S(1)}, f32[512,128]{1,0:T(8,128)S(1)}, u32[]{:S(2)}, u32[]{:S(2)}) collective-permute-start(f32[512,128]{1,0:T(8,128)S(1)} %add_add_fusion.2), channel_id=1, source_target_pairs={{0,28},{1,29},{2,30},{3,31},{12,8},{13,9},{14,10},{15,11},{32,60},... | collective-permute-start | bytes 786440 | tf_op jit(solution)/shard_map/ppermute | solution.py:21
  52.3 1.3 collective-permute-start.26
  55.0 12.7 %collective-permute-done.25.other = f32[384,128]{1,0:T(8,128)S(1)} collective-permute-done((f32[384,128]{1,0:T(8,128)S(1)}, f32[384,128]{1,0:T(8,128)S(1)}, u32[]{:S(2)}, u32[]{:S(2)}) %collective-permute-start.25) | collective-permute-done | bytes 196640 | tf_op jit(solution)/shard_map/ppermute | solution.py:21
  67.7 1.3 collective-permute-start.32
  69.0 1.3 collective-permute-start.31
  71.7 2.7 %collective-permute-start.29 = (f32[1024,128]{1,0:T(8,128)S(1)}, f32[1024,128]{1,0:T(8,128)S(1)}, u32[]{:S(2)}, u32[]{:S(2)}) collective-permute-start(f32[1024,128]{1,0:T(8,128)S(1)} %collective-permute-done.21.refs_2_), channel_id=1, source_target_pairs={{0,28},{1,29},{2,30},{3,31},{4,0},{5,1},{6,2},{7,3},{8,4},{9,5},{1... | collective-permute-start | bytes 1572872 | tf_op jit(solution)/shard_map/ppermute | solution.py:21
  74.4 10.5 %factor_first.1 = (f32[256,256]{1,0:T(8,128)S(1)}, f32[256,256]{1,0:T(8,128)S(1)}) custom-call(f32[384,128]{1,0:T(8,128)S(1)} %add_add_fusion.3.mine, f32[384,128]{1,0:T(8,128)S(1)} %collective-permute-done.25.other), custom_call_target="tpu_custom_call" | custom-call | flops 60000002048 | bytes 1048576 | tf_op jit(solution)/shard_map/factor_first/pallas_call | solution.py:219
  85.0 3.3 %collective-permute-start.35 = (f32[512,128]{1,0:T(8,128)S(1)}, f32[512,128]{1,0:T(8,128)S(1)}, u32[]{:S(2)}, u32[]{:S(2)}) collective-permute-start(f32[512,128]{1,0:T(8,128)S(1)} %add_add_fusion.mine), channel_id=1, source_target_pairs={{0,32},{1,33},{2,34},{3,35},{4,36},{5,37},{6,38},{7,39},{8,40},{9,... | collective-permute-start | bytes 786440 | tf_op jit(solution)/shard_map/ppermute | solution.py:21
  88.4 1.3 collective-permute-start.40
  89.7 1.3 collective-permute-start.39
  91.0 1.3 collective-permute-start.38
  93.4 1.7 %collective-permute-start.34 = (f32[1024,128]{1,0:T(8,128)S(1)}, f32[1024,128]{1,0:T(8,128)S(1)}, u32[]{:S(2)}, u32[]{:S(2)}) collective-permute-start(f32[1024,128]{1,0:T(8,128)S(1)} %collective-permute-done.29.refs_4_), channel_id=1, source_target_pairs={{0,28},{1,29},{2,30},{3,31},{4,0},{5,1},{6,2},{7,3},{8,4},{9,5},{1... | collective-permute-start | bytes 1572872 | tf_op jit(solution)/shard_map/ppermute | solution.py:21
  95.1 12.9 %factor_second.1 = (f32[2,256,256]{2,1,0:T(8,128)S(1)}, f32[512,512]{1,0:T(8,128)S(1)}) custom-call(s32[2]{0:T(128)S(1)} %pad_add_fusion.place, f32[512,128]{1,0:T(8,128)S(1)} %add_add_fusion.mine, f32[512,128]{1,0:T(8,128)S(1)} %collective-permute-done.35.other, f32[256,256]{1,0:T(8,128)S(1)} %get-tuple-element.60.upper0, ...), custom_call_target="tpu_custom_call" | custom-call | flops 60000002048 | bytes 1048576 | tf_op jit(solution)/shard_map/factor_second/pallas_call | solution.py:232
  108.0 4.4 %collective-permute-done.38 = f32[1024,128]{1,0:T(8,128)S(1)} collective-permute-done((f32[1024,128]{1,0:T(8,128)S(1)}, f32[1024,128]{1,0:T(8,128)S(1)}, u32[]{:S(2)}, u32[]{:S(2)}) %collective-permute-start.38) | collective-permute-done | bytes 524320 | tf_op jit(solution)/shard_map/ppermute | solution.py:21
  113.3 1.9 %collective-permute-start.37 = (f32[512,128]{1,0:T(8,128)S(1)}, f32[512,128]{1,0:T(8,128)S(1)}, u32[]{:S(2)}, u32[]{:S(2)}) collective-permute-start(f32[512,128]{1,0:T(8,128)S(1)} %slice.80), channel_id=1, source_target_pairs={{0,28},{1,29},{2,30},{3,31},{4,0},{5,1},{6,2},{7,3},{8,4},{9,5},{1... | collective-permute-start | bytes 786440 | tf_op jit(solution)/shard_map/ppermute | solution.py:21
  116.4 4.9 %collective-permute-done.37.end1 = f32[512,128]{1,0:T(8,128)S(1)} collective-permute-done((f32[512,128]{1,0:T(8,128)S(1)}, f32[512,128]{1,0:T(8,128)S(1)}, u32[]{:S(2)}, u32[]{:S(2)}) %collective-permute-start.37) | collective-permute-done | bytes 262176 | tf_op jit(solution)/shard_map/ppermute | solution.py:21
  121.3 2.7 %collective-permute-done.36.end0 = f32[512,128]{1,0:T(8,128)S(1)} collective-permute-done((f32[512,128]{1,0:T(8,128)S(1)}, f32[512,128]{1,0:T(8,128)S(1)}, u32[]{:S(2)}, u32[]{:S(2)}) %collective-permute-start.36) | collective-permute-done | bytes 262176 | tf_op jit(solution)/shard_map/ppermute | solution.py:21
  123.9 11.0 %update.1 = f32[8192,128]{1,0:T(8,128)} custom-call(s32[2]{0:T(128)S(1)} %pad_add_fusion.place, f32[8192,128]{1,0:T(8,128)S(1)} %bitcast.13, bf16[2048,512]{1,0:T(8,128)(2,1)S(1)} %get-tuple-element.68.high, bf16[2048,512]{1,0:T(8,128)(2,1)S(1)} %get-tuple-element.69.low, f32[512,128]{1,0:T(8,128)S(1)} %collective-permute-done.36.end0, ...), custom_call_target="tpu_custom_call" | custom-call | flops 8000000000 | bytes 16777216 | tf_op jit(solution)/shard_map/update/pallas_call | solution.py:354
  (87 shorter events, 19.7 us)
Async XLA Ops:
  1.5 17.0 %collective-permute-start.1 = (f32[256,128]{1,0:T(8,128)S(1)}, f32[256,128]{1,0:T(8,128)S(1)}, u32[]{:S(2)}, u32[]{:S(2)}) collective-permute-start(f32[256,128]{1,0:T(8,128)S(1)} %bitcast.32), channel_id=1, source_target_pairs={{0,1},{32,3},{1,33},{33,35},{2,65},{34,67},{3,97},{35,99},{4,133},... | collective-permute-start | bytes 393224 | tf_op jit(solution)/shard_map/ppermute | solution.py:21
  7.5 11.7 %collective-permute-start = (f32[256,128]{1,0:T(8,128)S(1)}, f32[256,128]{1,0:T(8,128)S(1)}, u32[]{:S(2)}, u32[]{:S(2)}) collective-permute-start(f32[256,128]{1,0:T(8,128)S(1)} %bitcast.31), channel_id=1, source_target_pairs={{0,0},{32,2},{1,32},{33,34},{2,64},{34,66},{3,96},{35,98},{4,132},... | collective-permute-start | bytes 393224 | tf_op jit(solution)/shard_map/ppermute | solution.py:21
  11.0 8.9 %collective-permute-start.2 = (f32[256,128]{1,0:T(8,128)S(1)}, f32[256,128]{1,0:T(8,128)S(1)}, u32[]{:S(2)}, u32[]{:S(2)}) collective-permute-start(f32[256,128]{1,0:T(8,128)S(1)} %bitcast.30), channel_id=1, source_target_pairs={{0,2},{32,0},{1,34},{33,32},{2,66},{34,64},{3,98},{35,96},{4,134},... | collective-permute-start | bytes 393224 | tf_op jit(solution)/shard_map/ppermute | solution.py:21
  21.4 7.5 %collective-permute-start.17 = (f32[512,128]{1,0:T(8,128)S(1)}, f32[512,128]{1,0:T(8,128)S(1)}, u32[]{:S(2)}, u32[]{:S(2)}) collective-permute-start(f32[512,128]{1,0:T(8,128)S(1)} %bitcast.23), channel_id=1, source_target_pairs={{1,3},{33,35}} | collective-permute-start | bytes 786440 | tf_op jit(solution)/shard_map/ppermute | solution.py:21
  22.1 9.0 %collective-permute-start.16 = (f32[512,128]{1,0:T(8,128)S(1)}, f32[512,128]{1,0:T(8,128)S(1)}, u32[]{:S(2)}, u32[]{:S(2)}) collective-permute-start(f32[512,128]{1,0:T(8,128)S(1)} %bitcast.24), channel_id=1, source_target_pairs={{1,0},{33,32}} | collective-permute-start | bytes 786440 | tf_op jit(solution)/shard_map/ppermute | solution.py:21
  23.4 7.7 %collective-permute-start.15 = (f32[512,128]{1,0:T(8,128)S(1)}, f32[512,128]{1,0:T(8,128)S(1)}, u32[]{:S(2)}, u32[]{:S(2)}) collective-permute-start(f32[512,128]{1,0:T(8,128)S(1)} %bitcast.25), channel_id=1, source_target_pairs={{1,2},{33,34}} | collective-permute-start | bytes 786440 | tf_op jit(solution)/shard_map/ppermute | solution.py:21
  24.1 13.0 %collective-permute-start.4 = (f32[256,128]{1,0:T(8,128)S(1)}, f32[256,128]{1,0:T(8,128)S(1)}, u32[]{:S(2)}, u32[]{:S(2)}) collective-permute-start(f32[256,128]{1,0:T(8,128)S(1)} %pad_maximum_fusion.2), channel_id=1, source_target_pairs={{0,4},{1,5},{2,6},{3,7},{8,12},{9,13},{10,14},{11,15},{16,20},{17,... | collective-permute-start | bytes 393224 | tf_op jit(solution)/shard_map/ppermute | solution.py:21
  28.2 8.9 %collective-permute-start.11 = (f32[384,128]{1,0:T(8,128)S(1)}, f32[384,128]{1,0:T(8,128)S(1)}, u32[]{:S(2)}, u32[]{:S(2)}) collective-permute-start(f32[384,128]{1,0:T(8,128)S(1)} %add_add_fusion.5), channel_id=1, source_target_pairs={{0,28},{1,29},{2,30},{3,31},{12,8},{13,9},{14,10},{15,11}} | collective-permute-start | bytes 589832 | tf_op jit(solution)/shard_map/ppermute | solution.py:21
  28.9 8.3 %collective-permute-start.10 = (f32[384,128]{1,0:T(8,128)S(1)}, f32[384,128]{1,0:T(8,128)S(1)}, u32[]{:S(2)}, u32[]{:S(2)}) collective-permute-start(f32[384,128]{1,0:T(8,128)S(1)} %add_add_fusion.5), channel_id=1, source_target_pairs={{0,4},{1,5},{2,6},{3,7},{12,16},{13,17},{14,18},{15,19},{20,24},{2... | collective-permute-start | bytes 589832 | tf_op jit(solution)/shard_map/ppermute | solution.py:21
  31.2 10.0 %collective-permute-start.19 = (f32[512,128]{1,0:T(8,128)S(1)}, f32[512,128]{1,0:T(8,128)S(1)}, u32[]{:S(2)}, u32[]{:S(2)}) collective-permute-start(f32[512,128]{1,0:T(8,128)S(1)} %add_select_fusion.1), channel_id=1, source_target_pairs={{0,20},{1,21},{2,22},{3,23},{32,52},{33,53},{34,54},{35,55}} | collective-permute-start | bytes 786440 | tf_op jit(solution)/shard_map/ppermute | solution.py:21
  37.2 11.9 %collective-permute-start.24 = (f32[384,128]{1,0:T(8,128)S(1)}, f32[384,128]{1,0:T(8,128)S(1)}, u32[]{:S(2)}, u32[]{:S(2)}) collective-permute-start(f32[384,128]{1,0:T(8,128)S(1)} %add_add_fusion.4), channel_id=1, source_target_pairs={{0,128},{1,129},{2,130},{3,131},{4,132},{5,133},{6,134},{7,135},{8... | collective-permute-start | bytes 589832 | tf_op jit(solution)/shard_map/ppermute | solution.py:21
  37.9 14.4 %collective-permute-start.23 = (f32[384,128]{1,0:T(8,128)S(1)}, f32[384,128]{1,0:T(8,128)S(1)}, u32[]{:S(2)}, u32[]{:S(2)}) collective-permute-start(f32[384,128]{1,0:T(8,128)S(1)} %add_add_fusion.4), channel_id=1, source_target_pairs={{0,192},{1,193},{2,194},{3,195},{4,196},{5,197},{6,198},{7,199},{8... | collective-permute-start | bytes 589832 | tf_op jit(solution)/shard_map/ppermute | solution.py:21
  43.9 9.7 %collective-permute-start.22 = (f32[384,128]{1,0:T(8,128)S(1)}, f32[384,128]{1,0:T(8,128)S(1)}, u32[]{:S(2)}, u32[]{:S(2)}) collective-permute-start(f32[384,128]{1,0:T(8,128)S(1)} %add_add_fusion.4), channel_id=1, source_target_pairs={{0,64},{1,65},{2,66},{3,67},{4,68},{5,69},{6,70},{7,71},{8,72},{9,... | collective-permute-start | bytes 589832 | tf_op jit(solution)/shard_map/ppermute | solution.py:21
  47.5 20.1 %collective-permute-start.21 = (f32[1024,128]{1,0:T(8,128)S(1)}, f32[1024,128]{1,0:T(8,128)S(1)}, u32[]{:S(2)}, u32[]{:S(2)}) collective-permute-start(f32[1024,128]{1,0:T(8,128)S(1)} %pad_maximum_fusion.refs_0_), channel_id=1, source_target_pairs={{0,28},{1,29},{2,30},{3,31},{4,0},{5,1},{6,2},{7,3},{8,4},{9,5},{1... | collective-permute-start | bytes 1572872 | tf_op jit(solution)/shard_map/ppermute | solution.py:21
  47.6 20.0 %collective-permute-start.20 = (f32[1024,128]{1,0:T(8,128)S(1)}, f32[1024,128]{1,0:T(8,128)S(1)}, u32[]{:S(2)}, u32[]{:S(2)}) collective-permute-start(f32[1024,128]{1,0:T(8,128)S(1)} %pad_maximum_fusion.refs_0_), channel_id=1, source_target_pairs={{0,4},{1,5},{2,6},{3,7},{4,8},{5,9},{6,10},{7,11},{8,12},{9,13},{1... | collective-permute-start | bytes 1572872 | tf_op jit(solution)/shard_map/ppermute | solution.py:21
  49.1 18.6 %collective-permute-start.27 = (f32[512,128]{1,0:T(8,128)S(1)}, f32[512,128]{1,0:T(8,128)S(1)}, u32[]{:S(2)}, u32[]{:S(2)}) collective-permute-start(f32[512,128]{1,0:T(8,128)S(1)} %add_add_fusion.2), channel_id=1, source_target_pairs={{0,28},{1,29},{2,30},{3,31},{12,8},{13,9},{14,10},{15,11},{32,60},... | collective-permute-start | bytes 786440 | tf_op jit(solution)/shard_map/ppermute | solution.py:21
  52.3 15.3 %collective-permute-start.26 = (f32[512,128]{1,0:T(8,128)S(1)}, f32[512,128]{1,0:T(8,128)S(1)}, u32[]{:S(2)}, u32[]{:S(2)}) collective-permute-start(f32[512,128]{1,0:T(8,128)S(1)} %add_add_fusion.2), channel_id=1, source_target_pairs={{0,4},{1,5},{2,6},{3,7},{12,16},{13,17},{14,18},{15,19},{20,24},{2... | collective-permute-start | bytes 786440 | tf_op jit(solution)/shard_map/ppermute | solution.py:21
  53.7 14.0 %collective-permute-start.25 = (f32[384,128]{1,0:T(8,128)S(1)}, f32[384,128]{1,0:T(8,128)S(1)}, u32[]{:S(2)}, u32[]{:S(2)}) collective-permute-start(f32[384,128]{1,0:T(8,128)S(1)} %add_add_fusion.3.mine), channel_id=1, source_target_pairs={{0,32},{1,33},{2,34},{3,35},{4,36},{5,37},{6,38},{7,39},{8,40},{9,... | collective-permute-start | bytes 589832 | tf_op jit(solution)/shard_map/ppermute | solution.py:21
  67.7 17.2 %collective-permute-start.32 = (f32[512,128]{1,0:T(8,128)S(1)}, f32[512,128]{1,0:T(8,128)S(1)}, u32[]{:S(2)}, u32[]{:S(2)}) collective-permute-start(f32[512,128]{1,0:T(8,128)S(1)} %add_add_fusion.1), channel_id=1, source_target_pairs={{0,128},{1,129},{2,130},{3,131},{4,132},{5,133},{6,134},{7,135},{8... | collective-permute-start | bytes 786440 | tf_op jit(solution)/shard_map/ppermute | solution.py:21
  69.0 15.9 %collective-permute-start.31 = (f32[512,128]{1,0:T(8,128)S(1)}, f32[512,128]{1,0:T(8,128)S(1)}, u32[]{:S(2)}, u32[]{:S(2)}) collective-permute-start(f32[512,128]{1,0:T(8,128)S(1)} %add_add_fusion.1), channel_id=1, source_target_pairs={{0,192},{1,193},{2,194},{3,195},{4,196},{5,197},{6,198},{7,199},{8... | collective-permute-start | bytes 786440 | tf_op jit(solution)/shard_map/ppermute | solution.py:21
  70.3 14.6 %collective-permute-start.30 = (f32[512,128]{1,0:T(8,128)S(1)}, f32[512,128]{1,0:T(8,128)S(1)}, u32[]{:S(2)}, u32[]{:S(2)}) collective-permute-start(f32[512,128]{1,0:T(8,128)S(1)} %add_add_fusion.1), channel_id=1, source_target_pairs={{0,64},{1,65},{2,66},{3,67},{4,68},{5,69},{6,70},{7,71},{8,72},{9,... | collective-permute-start | bytes 786440 | tf_op jit(solution)/shard_map/ppermute | solution.py:21
  71.7 13.3 %collective-permute-start.28 = (f32[1024,128]{1,0:T(8,128)S(1)}, f32[1024,128]{1,0:T(8,128)S(1)}, u32[]{:S(2)}, u32[]{:S(2)}) collective-permute-start(f32[1024,128]{1,0:T(8,128)S(1)} %collective-permute-done.20.refs_1_), channel_id=1, source_target_pairs={{0,4},{1,5},{2,6},{3,7},{4,8},{5,9},{6,10},{7,11},{8,12},{9,13},{1... | collective-permute-start | bytes 1572872 | tf_op jit(solution)/shard_map/ppermute | solution.py:21
  71.7 13.2 %collective-permute-start.29 = (f32[1024,128]{1,0:T(8,128)S(1)}, f32[1024,128]{1,0:T(8,128)S(1)}, u32[]{:S(2)}, u32[]{:S(2)}) collective-permute-start(f32[1024,128]{1,0:T(8,128)S(1)} %collective-permute-done.21.refs_2_), channel_id=1, source_target_pairs={{0,28},{1,29},{2,30},{3,31},{4,0},{5,1},{6,2},{7,3},{8,4},{9,5},{1... | collective-permute-start | bytes 1572872 | tf_op jit(solution)/shard_map/ppermute | solution.py:21
  85.0 8.4 %collective-permute-start.35 = (f32[512,128]{1,0:T(8,128)S(1)}, f32[512,128]{1,0:T(8,128)S(1)}, u32[]{:S(2)}, u32[]{:S(2)}) collective-permute-start(f32[512,128]{1,0:T(8,128)S(1)} %add_add_fusion.mine), channel_id=1, source_target_pairs={{0,32},{1,33},{2,34},{3,35},{4,36},{5,37},{6,38},{7,39},{8,40},{9,... | collective-permute-start | bytes 786440 | tf_op jit(solution)/shard_map/ppermute | solution.py:21
  88.4 19.6 %collective-permute-start.40 = (f32[1024,128]{1,0:T(8,128)S(1)}, f32[1024,128]{1,0:T(8,128)S(1)}, u32[]{:S(2)}, u32[]{:S(2)}) collective-permute-start(f32[1024,128]{1,0:T(8,128)S(1)} %bitcast.14), channel_id=1, source_target_pairs={{0,128},{1,129},{2,130},{3,131},{4,132},{5,133},{6,134},{7,135},{8... | collective-permute-start | bytes 1572872 | tf_op jit(solution)/shard_map/ppermute | solution.py:21
  89.7 18.3 %collective-permute-start.39 = (f32[1024,128]{1,0:T(8,128)S(1)}, f32[1024,128]{1,0:T(8,128)S(1)}, u32[]{:S(2)}, u32[]{:S(2)}) collective-permute-start(f32[1024,128]{1,0:T(8,128)S(1)} %bitcast.15), channel_id=1, source_target_pairs={{0,192},{1,193},{2,194},{3,195},{4,196},{5,197},{6,198},{7,199},{8... | collective-permute-start | bytes 1572872 | tf_op jit(solution)/shard_map/ppermute | solution.py:21
  91.0 21.4 %collective-permute-start.38 = (f32[1024,128]{1,0:T(8,128)S(1)}, f32[1024,128]{1,0:T(8,128)S(1)}, u32[]{:S(2)}, u32[]{:S(2)}) collective-permute-start(f32[1024,128]{1,0:T(8,128)S(1)} %bitcast.16), channel_id=1, source_target_pairs={{0,64},{1,65},{2,66},{3,67},{4,68},{5,69},{6,70},{7,71},{8,72},{9,... | collective-permute-start | bytes 1572872 | tf_op jit(solution)/shard_map/ppermute | solution.py:21
  92.4 20.8 %collective-permute-start.33 = (f32[1024,128]{1,0:T(8,128)S(1)}, f32[1024,128]{1,0:T(8,128)S(1)}, u32[]{:S(2)}, u32[]{:S(2)}) collective-permute-start(f32[1024,128]{1,0:T(8,128)S(1)} %collective-permute-done.28.refs_3_), channel_id=1, source_target_pairs={{0,4},{1,5},{2,6},{3,7},{4,8},{5,9},{6,10},{7,11},{8,12},{9,13},{1... | collective-permute-start | bytes 1572872 | tf_op jit(solution)/shard_map/ppermute | solution.py:21
  93.4 19.8 %collective-permute-start.34 = (f32[1024,128]{1,0:T(8,128)S(1)}, f32[1024,128]{1,0:T(8,128)S(1)}, u32[]{:S(2)}, u32[]{:S(2)}) collective-permute-start(f32[1024,128]{1,0:T(8,128)S(1)} %collective-permute-done.29.refs_4_), channel_id=1, source_target_pairs={{0,28},{1,29},{2,30},{3,31},{4,0},{5,1},{6,2},{7,3},{8,4},{9,5},{1... | collective-permute-start | bytes 1572872 | tf_op jit(solution)/shard_map/ppermute | solution.py:21
  112.5 11.4 %collective-permute-start.41 = (f32[1024,128]{1,0:T(8,128)S(1)}, f32[1024,128]{1,0:T(8,128)S(1)}, u32[]{:S(2)}, u32[]{:S(2)}) collective-permute-start(f32[1024,128]{1,0:T(8,128)S(1)} %add_select_fusion.mine), channel_id=1, source_target_pairs={{0,32},{1,33},{2,34},{3,35},{4,36},{5,37},{6,38},{7,39},{8,40},{9,... | collective-permute-start | bytes 1572872 | tf_op jit(solution)/shard_map/ppermute | solution.py:21
  113.3 8.0 %collective-permute-start.37 = (f32[512,128]{1,0:T(8,128)S(1)}, f32[512,128]{1,0:T(8,128)S(1)}, u32[]{:S(2)}, u32[]{:S(2)}) collective-permute-start(f32[512,128]{1,0:T(8,128)S(1)} %slice.80), channel_id=1, source_target_pairs={{0,28},{1,29},{2,30},{3,31},{4,0},{5,1},{6,2},{7,3},{8,4},{9,5},{1... | collective-permute-start | bytes 786440 | tf_op jit(solution)/shard_map/ppermute | solution.py:21
  115.1 8.8 %collective-permute-start.36 = (f32[512,128]{1,0:T(8,128)S(1)}, f32[512,128]{1,0:T(8,128)S(1)}, u32[]{:S(2)}, u32[]{:S(2)}) collective-permute-start(f32[512,128]{1,0:T(8,128)S(1)} %slice.79), channel_id=1, source_target_pairs={{0,4},{1,5},{2,6},{3,7},{4,8},{5,9},{6,10},{7,11},{8,12},{9,13},{1... | collective-permute-start | bytes 786440 | tf_op jit(solution)/shard_map/ppermute | solution.py:21
  (11 other events, 54.8 us)
